TPU v7x, 512 devices: a whole 4x8x8 slice. The times are simulated.
512 devices in a mesh: ctx: 64 (over x, z, core), head: 8 (over y).
Axes of the slice: x: 4, y: 8, z: 8, core: 2. Of those that a mesh axis runs over, the one named last changes fastest.
Arguments:
- values: bfloat16 [8192, 4096], P('ctx', 'head'), may hold values from -6 to 6
- gate_input: bfloat16 [8192, 4096], P('ctx', 'head'), may hold values from -6 to 6
- write_proj: bfloat16 [8192, 128], P('ctx'), may hold values from -0.5 to 0.5
- read_proj: bfloat16 [8192, 128], P('ctx'), may hold values from -6 to 6
- log_decay: float32 [64, 8192], P('head', 'ctx'), may hold values from -1 to 0
- level_logit: float32 [8, 64, 8192], P(None, 'head', 'ctx'), may hold values from -8 to 2
- norm_gain: float32 [4096], P('head'), may hold values from 0.25 to 1.75
- cotangent: bfloat16 [8192, 4096], P('ctx', 'head'), may hold values from -6 to 6
- final_cotangent: float32 [64, 8192], P('head', 'ctx'), may hold values from -6 to 6
Outputs:
- mixed: bfloat16 [8192, 4096], P('ctx', 'head')
- grad_values: bfloat16 [8192, 4096], P('ctx', 'head')
- grad_gating: bfloat16 [8192, 4096], P('ctx', 'head')
- grad_write: float32 [8192, 128], P('ctx')
- grad_read: float32 [8192, 128], P('ctx')
- grad_decay: float32 [64, 8192], P('head', 'ctx')
- grad_levels: float32 [8, 64, 8192], P(None, 'head', 'ctx')
- final_state: float32 [64, 8192], P('head', 'ctx')
All inputs are finite; a program needn't handle non-finite values.
Results may differ from a plain program's by a relative error of at most 0.0017.
Values sent between devices are 32-bit elements; how exact they have to be, the bound alone decides.
A program may use at most 128 MiB of HBM per device.

v0:
```python
import jax
import jax.numpy as jnp
from jax import lax
from jax.sharding import PartitionSpec as P

BLOCK = 64


epsilon = 1e-05
highest = lax.Precision.HIGHEST


def swapped(shard, axis, apart):
    return lax.ppermute(shard, axis, [(i, i ^ 1 << apart) for i in range(lax.axis_size(axis))])


def build_masks(rows, block_size, local_levels):
    positions = jnp.arange(rows)
    is_later = positions[:, None] >= positions[None, :]
    row_block = positions[:, None] // block_size
    column_block = positions[None, :] // block_size
    level_index = (row_block != column_block).astype(jnp.int32)
    level_index = level_index + (row_block // 2**1 != column_block // 2**1).astype(jnp.int32)
    layers = [
        jnp.where(is_later & (level_index == depth), 1.0, 0.0) for depth in range(local_levels + 1)
    ]
    return (jnp.stack(layers).astype(jnp.float32), is_later)


def shards(
    values,
    gate_input,
    write_proj,
    read_proj,
    log_decay,
    level_logit,
    norm_gain,
    cotangent,
    final_cotangent,
):
    rows = values.shape[0]
    heads = log_decay.shape[0]
    width = values.shape[1] // heads
    state_size = write_proj.shape[1]
    local_levels = (rows // BLOCK).bit_length() - 1
    ctx_count = lax.axis_size("ctx")
    cross_levels = ctx_count.bit_length() - 1
    all_channels = values.shape[1] * lax.axis_size("head")
    per_head = state_size * width
    slice_len = per_head // ctx_count
    final_scale = (state_size / (rows * ctx_count)) ** 0.5
    masks, is_later = build_masks(rows, BLOCK, local_levels)
    value_rows = values.astype(jnp.float32).reshape(rows, heads, width)
    write_rows = write_proj.astype(jnp.float32)
    read_rows = read_proj.astype(jnp.float32)
    weights_all = jnp.exp(level_logit)
    cumulative = jnp.cumsum(log_decay, axis=1)
    scores = jnp.dot(read_rows, write_rows.T, precision=highest)

    def head_scores(head):
        cum_head = cumulative[head]
        differ = cum_head[:, None] - cum_head[None, :]
        decay = jnp.exp(jnp.where(is_later, differ, 0.0))
        mixing = jnp.einsum(
            "lt,lts->ts", weights_all[: local_levels + 1, head], masks, precision=highest
        )
        return (mixing, decay)

    def local_forward(head):
        mixing, decay = head_scores(head)
        kernel = mixing * decay * scores
        return jnp.dot(kernel, value_rows[:, head], precision=highest)

    local_out = lax.map(local_forward, jnp.arange(heads))
    totals = cumulative[:, -1]
    fade = jnp.exp(totals[:, None] - cumulative)
    faded = value_rows * fade.T[:, :, None]
    ends = jnp.einsum("tn,thp->hnp", write_rows, faded, precision=highest)
    ctx_index = lax.axis_index("ctx")
    levels = []
    block, block_decay = (ends, totals)
    offset = jnp.zeros_like(totals)
    for depth in range(cross_levels):
        upper = (ctx_index // 2**depth % 2).astype(jnp.float32)
        partner, partner_decay = swapped((block, block_decay), "ctx", depth)
        levels.append((block, block_decay, partner, partner_decay, offset, upper))
        new_block = jnp.where(
            upper > 0.5,
            partner * jnp.exp(block_decay)[:, None, None] + block,
            block * jnp.exp(partner_decay)[:, None, None] + partner,
        )
        if depth + 1 < cross_levels:
            offset = offset + upper * partner_decay
        block_decay = block_decay + partner_decay
        block = new_block
    final_state = (
        lax.dynamic_slice_in_dim(
            block.reshape(heads, per_head), ctx_index * slice_len, slice_len, 1
        )
        * final_scale
    )
    cross_out = jnp.zeros((rows, heads, width), jnp.float32)
    for depth in range(cross_levels):
        partner, offset, upper = (levels[depth][2], levels[depth][4], levels[depth][5])
        weight = weights_all[1 + local_levels + depth] * jnp.exp(offset[:, None] + cumulative)
        projected = jnp.einsum("tn,hnp->thp", read_rows, partner * upper, precision=highest)
        cross_out = cross_out + weight.T[:, :, None] * projected
    mixed_rows = (jnp.transpose(local_out, (1, 0, 2)) + cross_out).reshape(rows, heads * width)
    gate_rows = gate_input.astype(jnp.float32)
    sigma = jax.nn.sigmoid(gate_rows)
    silu_gate = gate_rows * sigma
    gated = mixed_rows * silu_gate
    square_sum = lax.psum(jnp.sum(gated * gated, axis=1), "head")
    inverse = lax.rsqrt(square_sum / all_channels + epsilon)[:, None]
    normed = gated * inverse
    mixed = (normed * norm_gain).astype(jnp.bfloat16)
    scaled = cotangent.astype(jnp.float32) * norm_gain
    inner = lax.psum(jnp.sum(scaled * normed, axis=1), "head")
    grad_gated = inverse * (scaled - normed * (inner / all_channels)[:, None])
    grad_mixed = grad_gated * silu_gate
    grad_gating = (grad_gated * mixed_rows * sigma * (1.0 + gate_rows * (1.0 - sigma))).astype(
        jnp.bfloat16
    )
    grad_rows = grad_mixed.reshape(rows, heads, width)
    grad_read = jnp.zeros((rows, state_size), jnp.float32)
    grad_cum = jnp.zeros_like(cumulative)
    grad_states = []
    grad_offsets = []
    level_grads = []
    for depth in range(cross_levels):
        partner, offset, upper = (levels[depth][2], levels[depth][4], levels[depth][5])
        state = partner * upper
        weight = weights_all[1 + local_levels + depth] * jnp.exp(offset[:, None] + cumulative)
        projected = jnp.einsum("tn,hnp->thp", read_rows, state, precision=highest)
        pulled = jnp.sum(grad_rows * projected, axis=2).T * weight
        level_grads.append(pulled)
        grad_cum = grad_cum + pulled
        weighted = grad_rows * weight.T[:, :, None]
        grad_read = grad_read + jnp.einsum("thp,hnp->tn", weighted, state, precision=highest)
        grad_states.append(
            jnp.einsum("tn,thp->hnp", read_rows, weighted, precision=highest) * upper
        )
        grad_offsets.append(jnp.sum(pulled, axis=1))
    final_grad = final_cotangent * final_scale
    grad_block = lax.dynamic_update_slice_in_dim(
        jnp.zeros((heads, per_head), jnp.float32), final_grad, ctx_index * slice_len, 1
    ).reshape(heads, state_size, width)
    grad_block_decay = jnp.zeros_like(totals)
    grad_offset = jnp.zeros_like(totals)
    for depth in reversed(range(cross_levels)):
        block, block_decay, partner, partner_decay, offset, upper = levels[depth]
        upper_grad = grad_block * jnp.exp(block_decay)[:, None, None]
        lower_grad = grad_block * jnp.exp(partner_decay)[:, None, None]
        own_block = upper * grad_block + (1.0 - upper) * lower_grad
        to_partner = upper * upper_grad + (1.0 - upper) * grad_block
        own_decay = grad_block_decay + upper * jnp.sum(upper_grad * partner, axis=(1, 2))
        partner_grad_decay = (
            grad_block_decay
            + (1.0 - upper) * jnp.sum(lower_grad * block, axis=(1, 2))
            + upper * grad_offset
        )
        grad_offset = grad_offset + grad_offsets[depth]
        to_partner = to_partner + grad_states[depth]
        back_block, back_decay = swapped((to_partner, partner_grad_decay), "ctx", depth)
        grad_block = own_block + back_block
        grad_block_decay = own_decay + back_decay
    spread = jnp.einsum("tn,hnp->thp", write_rows, grad_block, precision=highest)
    grad_value_ends = spread * fade.T[:, :, None]
    grad_write = jnp.einsum("thp,hnp->tn", faded, grad_block, precision=highest)
    fade_pull = jnp.sum(faded * spread, axis=2).T
    grad_total = grad_block_decay + jnp.sum(fade_pull, axis=1)
    grad_cum = grad_cum - fade_pull

    def local_backward(carry, head):
        mixing, decay = head_scores(head)
        kernel = mixing * decay * scores
        grad_head = grad_rows[:, head]
        grad_kernel = jnp.dot(grad_head, value_rows[:, head].T, precision=highest)
        grad_value = jnp.dot(kernel.T, grad_head, precision=highest)
        pulled_local = grad_kernel * kernel
        grad_cum_head = jnp.sum(pulled_local, axis=1) - jnp.sum(pulled_local, axis=0)
        grad_mixing = grad_kernel * decay * scores
        grad_level = weights_all[: local_levels + 1, head] * jnp.einsum(
            "lts,ts->lt", masks, grad_mixing, precision=highest
        )
        return (carry + grad_kernel * mixing * decay, (grad_value, grad_cum_head, grad_level))

    grad_scores, (grad_local_values, grad_local_cum, grad_local_levels) = lax.scan(
        local_backward, jnp.zeros((rows, rows), jnp.float32), jnp.arange(heads)
    )
    grad_read = grad_read + jnp.dot(grad_scores, write_rows, precision=highest)
    grad_write = grad_write + jnp.dot(grad_scores.T, read_rows, precision=highest)
    grad_cum = grad_cum + grad_local_cum
    grad_cum = grad_cum.at[:, -1].add(grad_total)
    grad_decay = jnp.cumsum(grad_cum[:, ::-1], axis=1)[:, ::-1]
    grad_write, grad_read = lax.psum((grad_write, grad_read), "head")
    grad_values = (
        (jnp.transpose(grad_local_values, (1, 0, 2)) + grad_value_ends)
        .reshape(rows, heads * width)
        .astype(jnp.bfloat16)
    )
    grad_levels = jnp.concatenate(
        [jnp.transpose(grad_local_levels, (1, 0, 2)), jnp.stack(level_grads)], axis=0
    )
    return (
        mixed,
        grad_values,
        grad_gating,
        grad_write,
        grad_read,
        grad_decay,
        grad_levels,
        final_state,
    )


def solution(mesh):
    return jax.shard_map(
        shards,
        mesh=mesh,
        in_specs=(
            P("ctx", "head"),
            P("ctx", "head"),
            P("ctx", None),
            P("ctx", None),
            P("head", "ctx"),
            P(None, "head", "ctx"),
            P("head"),
            P("ctx", "head"),
            P("head", "ctx"),
        ),
        out_specs=(
            P("ctx", "head"),
            P("ctx", "head"),
            P("ctx", "head"),
            P("ctx", None),
            P("ctx", None),
            P("head", "ctx"),
            P(None, "head", "ctx"),
            P("head", "ctx"),
        ),
        check_vma=False,
    )
```

profile of v0, /device:TPU:1, one launch (start us, length us, event | category | flops | bytes accessed | tf_op | source)
XLA Modules:
  0.0 441.4 jit_solution(15625353134610348984)
XLA Ops:
  8.4 8.8 %collective-permute-start.1 = (f32[8]{0:T(128)S(1)}, f32[8]{0:T(128)S(1)}, u32[]{:S(2)}, u32[]{:S(2)}) collective-permute-start(f32[8]{0:T(128)S(1)} %slice_reduce_fusion), channel_id=1, source_target_pairs={{0,8},{8,0},{16,24},{24,16},{32,40},{40,32},{48,56},{56,48},{64,72... | collective-permute-start | bytes 104 | tf_op jit(solution)/shard_map/ppermute | solution.py:14
  27.7 5.3 %collective-permute-start.7 = (f32[8]{0:T(128)S(1)}, f32[8]{0:T(128)S(1)}, u32[]{:S(2)}, u32[]{:S(2)}) collective-permute-start(f32[8]{0:T(128)S(1)} %get-tuple-element.356), channel_id=1, source_target_pairs={{0,64},{8,72},{16,80},{24,88},{32,96},{40,104},{48,112},{56,120},{... | collective-permute-start | bytes 104 | tf_op jit(solution)/shard_map/ppermute | solution.py:14
  41.8 6.6 %collective-permute-start = (f32[8,128,64]{1,2,0:T(8,128)S(1)}, f32[8,128,64]{1,2,0:T(8,128)S(1)}, u32[]{:S(2)}, u32[]{:S(2)}) collective-permute-start(f32[8,128,64]{1,2,0:T(8,128)S(1)} %convolution_bitcast_fusion.9), channel_id=1, source_target_pairs={{0,8},{8,0},{16,24},{24,16},{32,40},{40,32},{48,56},{56,48},{64,72... | collective-permute-start | bytes 786440 | tf_op jit(solution)/shard_map/ppermute | solution.py:14
  52.0 7.1 %collective-permute-done.2 = f32[8,128,64]{1,2,0:T(8,128)S(1)} collective-permute-done((f32[8,128,64]{1,2,0:T(8,128)S(1)}, f32[8,128,64]{1,2,0:T(8,128)S(1)}, u32[]{:S(2)}, u32[]{:S(2)}) %collective-permute-start.2) | collective-permute-done | bytes 262176 | tf_op jit(solution)/shard_map/ppermute | solution.py:14
  61.2 32.7 %while.29 = (s32[]{:T(128)}, f32[8,128,64]{1,2,0:T(8,128)S(1)}, s32[8]{0:T(128)S(1)}, f32[8,8,128]{2,1,0:T(8,128)S(1)}, f32[2,128,128]{2,1,0:T(8,128)S(1)}, /*in...) while((s32[]{:T(128)}, f32[8,128,64]{1,2,0:T(8,128)S(1)}, ...), condition=%wide.region_2.3_spmd.clone, body=%wide.region_1.2_spmd.clone.sunk | while | flops 13058053 | bytes 498859 | solution.py:74
  94.7 7.5 %collective-permute-start.6 = (f32[8,128,64]{1,2,0:T(8,128)S(1)}, f32[8,128,64]{1,2,0:T(8,128)S(1)}, u32[]{:S(2)}, u32[]{:S(2)}) collective-permute-start(f32[8,128,64]{1,2,0:T(8,128)S(1)} %add_select_fusion.3), channel_id=1, source_target_pairs={{0,64},{8,72},{16,80},{24,88},{32,96},{40,104},{48,112},{56,120},{... | collective-permute-start | bytes 786440 | tf_op jit(solution)/shard_map/ppermute | solution.py:14
  102.8 4.7 %collective-permute-start.11 = (f32[8]{0:T(128)S(1)}, f32[8]{0:T(128)S(1)}, u32[]{:S(2)}, u32[]{:S(2)}) collective-permute-start(f32[8]{0:T(128)S(1)} %get-tuple-element.347), channel_id=1, source_target_pairs={{0,256},{8,264},{16,272},{24,280},{32,288},{40,296},{48,304},{56,3... | collective-permute-start | bytes 104 | tf_op jit(solution)/shard_map/ppermute | solution.py:14
  113.6 3.4 collective-permute-done.8
  117.2 4.7 %collective-permute-start.10 = (f32[8,128,64]{1,2,0:T(8,128)S(1)}, f32[8,128,64]{1,2,0:T(8,128)S(1)}, u32[]{:S(2)}, u32[]{:S(2)}) collective-permute-start(f32[8,128,64]{1,2,0:T(8,128)S(1)} %add_select_fusion.1), channel_id=1, source_target_pairs={{0,256},{8,264},{16,272},{24,280},{32,288},{40,296},{48,304},{56,3... | collective-permute-start | bytes 786440 | tf_op jit(solution)/shard_map/ppermute | solution.py:14
  128.3 13.9 %psum.28 = f32[128]{0:T(128)S(1)} all-reduce(f32[128]{0:T(128)S(1)} %multiply_reduce_fusion.21), channel_id=1, replica_groups=mesh['ctx'=64,'head'=8] {'head'}, use_global_device_ids=true, to_apply=%region_4.5 | all-reduce | flops 128 | bytes 1024 | tf_op jit(solution)/shard_map/psum | solution.py:113
  143.3 11.5 %psum.29 = f32[128]{0:T(128)S(1)} all-reduce(f32[128]{0:T(128)S(1)} %multiply_reduce_fusion.20), channel_id=1, replica_groups=mesh['ctx'=64,'head'=8] {'head'}, use_global_device_ids=true, to_apply=%region_6.7 | all-reduce | flops 128 | bytes 1024 | tf_op jit(solution)/shard_map/psum | solution.py:118
  160.7 108.9 %while.30 = (s32[]{:T(128)}, f32[128,128]{1,0:T(8,128)S(1)}, f32[8,128,64]{1,2,0:T(8,128)}, f32[8,128]{1,0:T(8,128)}, f32[8,2,128]{2,0,1:T(8,128)}, /*index=5*/s...) while((s32[]{:T(128)}, f32[128,128]{1,0:T(8,128)S(1)}, ...), condition=%wide.region_10.11_spmd.clone, body=%wide.region_7.10_spmd.clone.sunk | while | flops 26181764 | bytes 1889929 | solution.py:188
  271.8 4.6 %collective-permute-start.12 = (f32[8,128,64]{1,2,0:T(8,128)S(1)}, f32[8,128,64]{1,2,0:T(8,128)S(1)}, u32[]{:S(2)}, u32[]{:S(2)}) collective-permute-start(f32[8,128,64]{1,2,0:T(8,128)S(1)} %fusion.36), channel_id=1, source_target_pairs={{0,256},{8,264},{16,272},{24,280},{32,288},{40,296},{48,304},{56,3... | collective-permute-start | bytes 786440 | tf_op jit(solution)/shard_map/ppermute | solution.py:14
  286.9 3.4 collective-permute-done.13
  291.4 7.0 %collective-permute-start.14 = (f32[8,128,64]{1,2,0:T(8,128)S(1)}, f32[8,128,64]{1,2,0:T(8,128)S(1)}, u32[]{:S(2)}, u32[]{:S(2)}) collective-permute-start(f32[8,128,64]{1,2,0:T(8,128)S(1)} %add_add_fusion.6), channel_id=1, source_target_pairs={{0,64},{8,72},{16,80},{24,88},{32,96},{40,104},{48,112},{56,120},{... | collective-permute-start | bytes 786440 | tf_op jit(solution)/shard_map/ppermute | solution.py:14
  303.7 11.2 %collective-permute-start.15 = (f32[8,128,64]{1,2,0:T(8,128)S(1)}, f32[8,128,64]{1,2,0:T(8,128)S(1)}, u32[]{:S(2)}, u32[]{:S(2)}) collective-permute-start(f32[8,128,64]{1,2,0:T(8,128)S(1)} %add_add_fusion.4), channel_id=1, source_target_pairs={{0,32},{8,40},{16,48},{24,56},{32,0},{40,8},{48,16},{56,24},{64,96... | collective-permute-start | bytes 786440 | tf_op jit(solution)/shard_map/ppermute | solution.py:14
  315.8 7.1 %collective-permute-done.15 = f32[8,128,64]{1,2,0:T(8,128)S(1)} collective-permute-done((f32[8,128,64]{1,2,0:T(8,128)S(1)}, f32[8,128,64]{1,2,0:T(8,128)S(1)}, u32[]{:S(2)}, u32[]{:S(2)}) %collective-permute-start.15) | collective-permute-done | bytes 262176 | tf_op jit(solution)/shard_map/ppermute | solution.py:14
  323.9 7.8 %collective-permute-start.16 = (f32[8,128,64]{1,2,0:T(8,128)S(1)}, f32[8,128,64]{1,2,0:T(8,128)S(1)}, u32[]{:S(2)}, u32[]{:S(2)}) collective-permute-start(f32[8,128,64]{1,2,0:T(8,128)S(1)} %add_add_fusion.2), channel_id=1, source_target_pairs={{0,16},{8,24},{16,0},{24,8},{32,48},{40,56},{48,32},{56,40},{64,80... | collective-permute-start | bytes 786440 | tf_op jit(solution)/shard_map/ppermute | solution.py:14
  336.0 13.7 %collective-permute-start.17 = (f32[8,128,64]{1,2,0:T(8,128)S(1)}, f32[8,128,64]{1,2,0:T(8,128)S(1)}, u32[]{:S(2)}, u32[]{:S(2)}) collective-permute-start(f32[8,128,64]{1,2,0:T(8,128)S(1)} %add_add_fusion), channel_id=1, source_target_pairs={{0,8},{8,0},{16,24},{24,16},{32,40},{40,32},{48,56},{56,48},{64,72... | collective-permute-start | bytes 786440 | tf_op jit(solution)/shard_map/ppermute | solution.py:14
  349.7 4.2 collective-permute-start.18
  362.3 6.6 %collective-permute-start.20 = (f32[8]{0:T(128)S(1)}, f32[8]{0:T(128)S(1)}, u32[]{:S(2)}, u32[]{:S(2)}) collective-permute-start(f32[8]{0:T(128)S(1)} %get-tuple-element.342), channel_id=1, source_target_pairs={{0,64},{8,72},{16,80},{24,88},{32,96},{40,104},{48,112},{56,120},{... | collective-permute-start | bytes 104 | tf_op jit(solution)/shard_map/ppermute | solution.py:14
  376.9 3.6 collective-permute-start.22
  381.6 6.3 %collective-permute-start.23 = (f32[8]{0:T(128)S(1)}, f32[8]{0:T(128)S(1)}, u32[]{:S(2)}, u32[]{:S(2)}) collective-permute-start(f32[8]{0:T(128)S(1)} %get-tuple-element.332), channel_id=1, source_target_pairs={{0,8},{8,0},{16,24},{24,16},{32,40},{40,32},{48,56},{56,48},{64,72... | collective-permute-start | bytes 104 | tf_op jit(solution)/shard_map/ppermute | solution.py:14
  389.9 42.5 %all-reduce.3.cloned.1.call-done = (f32[128,128]{1,0:T(8,128)}, f32[128,128]{1,0:T(8,128)}) async-done(((f32[128,128]{1,0:T(8,128)}, f32[128,128]{1,0:T(8,128)}), (f32[128,128]{1,0:T(8,128)}, f32[128,128]{1,0:T(8,128)})) %all-reduce.3.cloned.1.call-update) | async-done | bytes 131088 | tf_op jit(solution)/shard_map/psum | solution.py:196
  (560 shorter events, 202.7 us)
Async XLA Ops:
  7.2 425.2 %all-reduce.3.cloned.1.call-start = ((), (), s32[]{:S(2)}) async-start(), calls=%async_computation | async-start | bytes 262144 | tf_op jit(solution)/shard_map/psum | solution.py:196
  8.4 9.8 %collective-permute-start.1 = (f32[8]{0:T(128)S(1)}, f32[8]{0:T(128)S(1)}, u32[]{:S(2)}, u32[]{:S(2)}) collective-permute-start(f32[8]{0:T(128)S(1)} %slice_reduce_fusion), channel_id=1, source_target_pairs={{0,8},{8,0},{16,24},{24,16},{32,40},{40,32},{48,56},{56,48},{64,72... | collective-permute-start | bytes 104 | tf_op jit(solution)/shard_map/ppermute | solution.py:14
  18.2 4.3 collective-permute-start.3
  22.5 5.2 %collective-permute-start.5 = (f32[8]{0:T(128)S(1)}, f32[8]{0:T(128)S(1)}, u32[]{:S(2)}, u32[]{:S(2)}) collective-permute-start(f32[8]{0:T(128)S(1)} %get-tuple-element.358), channel_id=1, source_target_pairs={{0,32},{8,40},{16,48},{24,56},{32,0},{40,8},{48,16},{56,24},{64,96... | collective-permute-start | bytes 104 | tf_op jit(solution)/shard_map/ppermute | solution.py:14
  27.7 8.2 %collective-permute-start.7 = (f32[8]{0:T(128)S(1)}, f32[8]{0:T(128)S(1)}, u32[]{:S(2)}, u32[]{:S(2)}) collective-permute-start(f32[8]{0:T(128)S(1)} %get-tuple-element.356), channel_id=1, source_target_pairs={{0,64},{8,72},{16,80},{24,88},{32,96},{40,104},{48,112},{56,120},{... | collective-permute-start | bytes 104 | tf_op jit(solution)/shard_map/ppermute | solution.py:14
  41.8 7.7 %collective-permute-start = (f32[8,128,64]{1,2,0:T(8,128)S(1)}, f32[8,128,64]{1,2,0:T(8,128)S(1)}, u32[]{:S(2)}, u32[]{:S(2)}) collective-permute-start(f32[8,128,64]{1,2,0:T(8,128)S(1)} %convolution_bitcast_fusion.9), channel_id=1, source_target_pairs={{0,8},{8,0},{16,24},{24,16},{32,40},{40,32},{48,56},{56,48},{64,72... | collective-permute-start | bytes 786440 | tf_op jit(solution)/shard_map/ppermute | solution.py:14
  49.7 9.4 %collective-permute-start.2 = (f32[8,128,64]{1,2,0:T(8,128)S(1)}, f32[8,128,64]{1,2,0:T(8,128)S(1)}, u32[]{:S(2)}, u32[]{:S(2)}) collective-permute-start(f32[8,128,64]{1,2,0:T(8,128)S(1)} %add_select_fusion.5), channel_id=1, source_target_pairs={{0,16},{8,24},{16,0},{24,8},{32,48},{40,56},{48,32},{56,40},{64,80... | collective-permute-start | bytes 786440 | tf_op jit(solution)/shard_map/ppermute | solution.py:14
  59.2 34.7 %collective-permute-start.4 = (f32[8,128,64]{1,2,0:T(8,128)S(1)}, f32[8,128,64]{1,2,0:T(8,128)S(1)}, u32[]{:S(2)}, u32[]{:S(2)}) collective-permute-start(f32[8,128,64]{1,2,0:T(8,128)S(1)} %add_select_fusion.4), channel_id=1, source_target_pairs={{0,32},{8,40},{16,48},{24,56},{32,0},{40,8},{48,16},{56,24},{64,96... | collective-permute-start | bytes 786440 | tf_op jit(solution)/shard_map/ppermute | solution.py:14
  94.7 15.0 %collective-permute-start.6 = (f32[8,128,64]{1,2,0:T(8,128)S(1)}, f32[8,128,64]{1,2,0:T(8,128)S(1)}, u32[]{:S(2)}, u32[]{:S(2)}) collective-permute-start(f32[8,128,64]{1,2,0:T(8,128)S(1)} %add_select_fusion.3), channel_id=1, source_target_pairs={{0,64},{8,72},{16,80},{24,88},{32,96},{40,104},{48,112},{56,120},{... | collective-permute-start | bytes 786440 | tf_op jit(solution)/shard_map/ppermute | solution.py:14
  102.8 6.1 %collective-permute-start.11 = (f32[8]{0:T(128)S(1)}, f32[8]{0:T(128)S(1)}, u32[]{:S(2)}, u32[]{:S(2)}) collective-permute-start(f32[8]{0:T(128)S(1)} %get-tuple-element.347), channel_id=1, source_target_pairs={{0,256},{8,264},{16,272},{24,280},{32,288},{40,296},{48,304},{56,3... | collective-permute-start | bytes 104 | tf_op jit(solution)/shard_map/ppermute | solution.py:14
  109.9 7.1 %collective-permute-start.8 = (f32[8,128,64]{1,2,0:T(8,128)S(1)}, f32[8,128,64]{1,2,0:T(8,128)S(1)}, u32[]{:S(2)}, u32[]{:S(2)}) collective-permute-start(f32[8,128,64]{1,2,0:T(8,128)S(1)} %add_select_fusion.2), channel_id=1, source_target_pairs={{0,128},{8,136},{16,144},{24,152},{32,160},{40,168},{48,176},{56,1... | collective-permute-start | bytes 786440 | tf_op jit(solution)/shard_map/ppermute | solution.py:14
  117.2 8.6 %collective-permute-start.10 = (f32[8,128,64]{1,2,0:T(8,128)S(1)}, f32[8,128,64]{1,2,0:T(8,128)S(1)}, u32[]{:S(2)}, u32[]{:S(2)}) collective-permute-start(f32[8,128,64]{1,2,0:T(8,128)S(1)} %add_select_fusion.1), channel_id=1, source_target_pairs={{0,256},{8,264},{16,272},{24,280},{32,288},{40,296},{48,304},{56,3... | collective-permute-start | bytes 786440 | tf_op jit(solution)/shard_map/ppermute | solution.py:14
  271.8 8.8 %collective-permute-start.12 = (f32[8,128,64]{1,2,0:T(8,128)S(1)}, f32[8,128,64]{1,2,0:T(8,128)S(1)}, u32[]{:S(2)}, u32[]{:S(2)}) collective-permute-start(f32[8,128,64]{1,2,0:T(8,128)S(1)} %fusion.36), channel_id=1, source_target_pairs={{0,256},{8,264},{16,272},{24,280},{32,288},{40,296},{48,304},{56,3... | collective-permute-start | bytes 786440 | tf_op jit(solution)/shard_map/ppermute | solution.py:14
  283.0 7.2 %collective-permute-start.13 = (f32[8,128,64]{1,2,0:T(8,128)S(1)}, f32[8,128,64]{1,2,0:T(8,128)S(1)}, u32[]{:S(2)}, u32[]{:S(2)}) collective-permute-start(f32[8,128,64]{1,2,0:T(8,128)S(1)} %add_add_fusion.8), channel_id=1, source_target_pairs={{0,128},{8,136},{16,144},{24,152},{32,160},{40,168},{48,176},{56,1... | collective-permute-start | bytes 786440 | tf_op jit(solution)/shard_map/ppermute | solution.py:14
  291.4 11.2 %collective-permute-start.14 = (f32[8,128,64]{1,2,0:T(8,128)S(1)}, f32[8,128,64]{1,2,0:T(8,128)S(1)}, u32[]{:S(2)}, u32[]{:S(2)}) collective-permute-start(f32[8,128,64]{1,2,0:T(8,128)S(1)} %add_add_fusion.6), channel_id=1, source_target_pairs={{0,64},{8,72},{16,80},{24,88},{32,96},{40,104},{48,112},{56,120},{... | collective-permute-start | bytes 786440 | tf_op jit(solution)/shard_map/ppermute | solution.py:14
  303.7 19.2 %collective-permute-start.15 = (f32[8,128,64]{1,2,0:T(8,128)S(1)}, f32[8,128,64]{1,2,0:T(8,128)S(1)}, u32[]{:S(2)}, u32[]{:S(2)}) collective-permute-start(f32[8,128,64]{1,2,0:T(8,128)S(1)} %add_add_fusion.4), channel_id=1, source_target_pairs={{0,32},{8,40},{16,48},{24,56},{32,0},{40,8},{48,16},{56,24},{64,96... | collective-permute-start | bytes 786440 | tf_op jit(solution)/shard_map/ppermute | solution.py:14
  323.9 11.6 %collective-permute-start.16 = (f32[8,128,64]{1,2,0:T(8,128)S(1)}, f32[8,128,64]{1,2,0:T(8,128)S(1)}, u32[]{:S(2)}, u32[]{:S(2)}) collective-permute-start(f32[8,128,64]{1,2,0:T(8,128)S(1)} %add_add_fusion.2), channel_id=1, source_target_pairs={{0,16},{8,24},{16,0},{24,8},{32,48},{40,56},{48,32},{56,40},{64,80... | collective-permute-start | bytes 786440 | tf_op jit(solution)/shard_map/ppermute | solution.py:14
  336.0 19.0 %collective-permute-start.17 = (f32[8,128,64]{1,2,0:T(8,128)S(1)}, f32[8,128,64]{1,2,0:T(8,128)S(1)}, u32[]{:S(2)}, u32[]{:S(2)}) collective-permute-start(f32[8,128,64]{1,2,0:T(8,128)S(1)} %add_add_fusion), channel_id=1, source_target_pairs={{0,8},{8,0},{16,24},{24,16},{32,40},{40,32},{48,56},{56,48},{64,72... | collective-permute-start | bytes 786440 | tf_op jit(solution)/shard_map/ppermute | solution.py:14
  349.7 6.7 %collective-permute-start.18 = (f32[8]{0:T(128)S(1)}, f32[8]{0:T(128)S(1)}, u32[]{:S(2)}, u32[]{:S(2)}) collective-permute-start(f32[8]{0:T(128)S(1)} %multiply_add_fusion.5), channel_id=1, source_target_pairs={{0,256},{8,264},{16,272},{24,280},{32,288},{40,296},{48,304},{56,3... | collective-permute-start | bytes 104 | tf_op jit(solution)/shard_map/ppermute | solution.py:14
  357.2 4.4 %collective-permute-start.19 = (f32[8]{0:T(128)S(1)}, f32[8]{0:T(128)S(1)}, u32[]{:S(2)}, u32[]{:S(2)}) collective-permute-start(f32[8]{0:T(128)S(1)} %multiply_add_fusion.4), channel_id=1, source_target_pairs={{0,128},{8,136},{16,144},{24,152},{32,160},{40,168},{48,176},{56,1... | collective-permute-start | bytes 104 | tf_op jit(solution)/shard_map/ppermute | solution.py:14
  362.3 8.2 %collective-permute-start.20 = (f32[8]{0:T(128)S(1)}, f32[8]{0:T(128)S(1)}, u32[]{:S(2)}, u32[]{:S(2)}) collective-permute-start(f32[8]{0:T(128)S(1)} %get-tuple-element.342), channel_id=1, source_target_pairs={{0,64},{8,72},{16,80},{24,88},{32,96},{40,104},{48,112},{56,120},{... | collective-permute-start | bytes 104 | tf_op jit(solution)/shard_map/ppermute | solution.py:14
  371.2 5.2 %collective-permute-start.21 = (f32[8]{0:T(128)S(1)}, f32[8]{0:T(128)S(1)}, u32[]{:S(2)}, u32[]{:S(2)}) collective-permute-start(f32[8]{0:T(128)S(1)} %get-tuple-element.338), channel_id=1, source_target_pairs={{0,32},{8,40},{16,48},{24,56},{32,0},{40,8},{48,16},{56,24},{64,96... | collective-permute-start | bytes 104 | tf_op jit(solution)/shard_map/ppermute | solution.py:14
  376.9 4.6 %collective-permute-start.22 = (f32[8]{0:T(128)S(1)}, f32[8]{0:T(128)S(1)}, u32[]{:S(2)}, u32[]{:S(2)}) collective-permute-start(f32[8]{0:T(128)S(1)} %get-tuple-element.335), channel_id=1, source_target_pairs={{0,16},{8,24},{16,0},{24,8},{32,48},{40,56},{48,32},{56,40},{64,80... | collective-permute-start | bytes 104 | tf_op jit(solution)/shard_map/ppermute | solution.py:14
  381.6 7.1 %collective-permute-start.23 = (f32[8]{0:T(128)S(1)}, f32[8]{0:T(128)S(1)}, u32[]{:S(2)}, u32[]{:S(2)}) collective-permute-start(f32[8]{0:T(128)S(1)} %get-tuple-element.332), channel_id=1, source_target_pairs={{0,8},{8,0},{16,24},{24,16},{32,40},{40,32},{48,56},{56,48},{64,72... | collective-permute-start | bytes 104 | tf_op jit(solution)/shard_map/ppermute | solution.py:14
  (134 other events, 1348.6 us)
Sparse Core Ops, SparseCore 0:
  361.7 70.6 all-reduce.2
where the time goes:
time: 449 us; the launch traced here: 441 us
  starting transfers between devices  122 us (27%)
  waiting for transfers between devices  91.6 us (20%)
  local copies, waits for them, and re-layouts  75.3 us (17%)
  matrix products  66.3 us (15%)
  loops' own time  31.9 us (7%)
  blocking collectives  25.4 us (6%)
  between operations  15.5 us (3%)
  other arithmetic  13.1 us (3%)
    ppermute x24, starting transfers between devices, swapped(): lax.ppermute(shard, axis, [(i, i ^ 1 << apart) for i in range(lax.axis_si...  122 us
    ppermute x24, waiting for transfers between devices, swapped(): lax.ppermute(shard, axis, [(i, i ^ 1 << apart) for i in range(lax.axis_si...  49.2 us
    psum x1, waiting for transfers between devices, shards(): grad_write, grad_read = lax.psum((grad_write, grad_read), 'head')  42.5 us
    dot_general x16, matrix products, head_scores(): jnp.einsum('lt,lts->ts', weights_all[:local_levels + 1, head], masks, pre...  28.3 us
    dynamic_update_slice x16, local copies, waits for them, and re-layouts, shards(): lax.scan(local_backward, jnp.zeros((rows, rows), jnp.float32), jnp.arange...  21 us
    while x96, local copies, waits for them, and re-layouts  16.3 us
    another operation x1, loops' own time, shards(): local_out = lax.map(local_forward, jnp.arange(heads))  16 us
    another operation x1, loops' own time, shards(): lax.scan(local_backward, jnp.zeros((rows, rows), jnp.float32), jnp.arange...  15.9 us
  transfers between devices with their start and end apart: 25, of which 18 were waited for; matrix products, arithmetic and copies ran while one was open for 7% of the time, Pallas kernels for 0%

commit v1 on v0

v1 whole, which is shorter than its diff:
```python
import functools

import jax
import jax.numpy as jnp
from jax import lax
from jax.experimental import pallas as pl
from jax.experimental.pallas import tpu as pltpu
from jax.sharding import PartitionSpec as P

F32 = jnp.float32
BF16 = jnp.bfloat16
EPSILON = 1e-05
BLOCK = 64
FAR = -1e30
NN = (((1,), (0,)), ((), ()))
NT = (((1,), (1,)), ((), ()))
TN = (((0,), (0,)), ((), ()))


def split(array):
    high = array.astype(BF16)
    return high, (array - high.astype(F32)).astype(BF16)


def mul(a, b, dims=NN):
    return lax.dot_general(a, b, dims, preferred_element_type=F32)


def left_two(a, b, dims=NN):
    high, low = split(a)
    return mul(high, b, dims) + mul(low, b, dims)


def right_two(a, b, dims=NN):
    high, low = split(b)
    return mul(a, high, dims) + mul(a, low, dims)


def both(a, b, dims=NN):
    a_high, a_low = split(a)
    b_high, b_low = split(b)
    return mul(a_high, b_high, dims) + (mul(a_low, b_high, dims) + mul(a_high, b_low, dims))


def exact(a, b, dims=NN):
    return lax.dot_general(
        a, b, dims, precision=lax.Precision.HIGHEST, preferred_element_type=F32
    )


def iota(shape, dim):
    return lax.broadcasted_iota(jnp.int32, shape, dim)


def layer(
    sizes,
    v_ref, g_ref, b_ref, r_ref, ld_ref, ll_ref, gain_ref, ct_ref, fc_ref,
    mixed_ref, gv_ref, gg_ref, gw_ref, gr_ref, gd_ref, gl_ref, fs_ref,
    fx, fd, own_e, core_e, s1h, zr, zs, xr, xs, st,
    wx, wp, md, ya, dl, dr, d0, dh, zb, xbs, xb, g1s, g1, gsc, gvl, gsm,
    t_own, t_core, t_pair, t_z, t_plane, t_x, f_own, f_x,
    v_own, v_core, v_pair, v_z, v_plane, v_x,
    n_own, n_y, part_r, rs_r, ag_r, own_r, part_w, rs_w, ag_w, own_w,
    core_send, core_recv, z_send, z_recv, x_send, x_recv, y_send, y_recv,
    down_send, down_recv, up_send, up_recv,
):
    X, Z, Y, T, N, H, width = sizes
    C = H * width
    SR = 2 * X
    half = Z * SR
    lz, lx = Z.bit_length() - 1, X.bit_length() - 1
    cross = 1 + lz + lx
    slots = lz + lx
    final_scale = (N / (T * X * Z * 2)) ** 0.5
    channels = C * Y

    me = lax.axis_index("ctx")
    y = lax.axis_index("head")
    k = me % 2
    z = (me // 2) % Z
    x = me // (2 * Z)
    kf = k.astype(F32)

    def device(x_, z_, k_, y_):
        return (x_ * (2 * Z) + z_ * 2 + k_, y_)

    core = device(x, z, 1 - k, y)
    zs_of = [(z + j) % Z for j in range(1, Z)]
    xs_of = [(x + j) % X for j in range(1, X)]
    ys_of = [(y + j) % Y for j in range(1, Y)]
    z_dev = [device(x, p, k, y) for p in zs_of]
    x_dev = [device(p, z, k, y) for p in xs_of]
    y_dev = [device(x, z, k, p) for p in ys_of]

    barrier = pltpu.get_barrier_semaphore()
    peers = [core] + z_dev + x_dev + y_dev
    for peer in peers:
        pl.semaphore_signal(barrier, inc=1, device_id=peer, device_id_type=pl.DeviceIdType.MESH)

    sent = []

    def copy(src, dst, send_sem, recv_sem, peer):
        return pltpu.make_async_remote_copy(
            src_ref=src, dst_ref=dst, send_sem=send_sem, recv_sem=recv_sem,
            device_id=peer, device_id_type=pl.DeviceIdType.MESH,
        )

    def send(src, dst, send_sem, recv_sem, peer, cond=None):
        item = copy(src, dst, send_sem, recv_sem, peer)
        if cond is None:
            item.start()
        else:
            pl.when(cond)(item.start)
        sent.append((item, cond))

    def recv(dst, send_sem, recv_sem, peer, cond=None):
        item = copy(dst, dst, send_sem, recv_sem, peer)
        if cond is None:
            item.wait_recv()
        else:
            pl.when(cond)(item.wait_recv)

    def bit(index, place):
        return (index // 2**place) % 2 == 1

    def needs(z_, slot):
        return bit(z_, slot) if slot < lz else bit(x, slot - lz)

    def rows(start, size):
        return pl.ds(pl.multiple_of(start, size), size)

    head_of = iota((H, C), 1) // width
    pick = head_of == iota((H, C), 0)
    pick16 = jnp.where(pick, 1.0, 0.0).astype(BF16)

    def wide(tile):
        many = jnp.concatenate([tile] * (C // 128), axis=1)
        return jnp.sum(jnp.where(pick, many, 0.0), axis=0, keepdims=True)

    def spread_out(array):
        return left_two(array, pick16, TN)

    j_ = iota((N, N), 0)
    n_ = iota((N, N), 1)
    natural = ((j_ % SR) // 2) * (4 * Z) + ((j_ % half) // SR) * 4 + (j_ // half) * 2 + j_ % 2
    order = jnp.where(natural == n_, 1.0, 0.0).astype(BF16)

    write = b_ref[...]
    read = r_ref[...]
    write_p = mul(write, order, NT).astype(BF16)
    write_t = mul(order, write, NT).astype(BF16)
    read_p = mul(read, order, NT).astype(BF16)
    read_t = mul(order, read, NT).astype(BF16)

    t_row = iota((T, T), 0)
    t_col = iota((T, T), 1)
    upto = jnp.where(t_row <= t_col, 1.0, 0.0)
    cum = exact(ld_ref[...], upto)
    total = jnp.broadcast_to(cum[:, T - 1:T], (H, 128))
    t_own[...] = total
    fade = jnp.exp(cum[:, T - 1:T] - cum)
    fx[...] = spread_out(fade)
    faded = v_ref[...].astype(F32) * fx[...]
    fd[...] = faded
    own_e[...] = right_two(write_t, faded)
    f_own[...] = fc_ref[...]

    @pl.when(k == 1)
    def _():
        d0[...] = jnp.zeros((N, C), F32)

    pl.semaphore_wait(barrier, len(peers))

    send(t_own, t_core, core_send.at[0], core_recv.at[0], core)
    send(own_e, core_e, core_send.at[1], core_recv.at[1], core)
    for j, p in enumerate(xs_of):
        send(f_own, f_x.at[x], x_send.at[0, j], x_recv.at[0, x], x_dev[j])

    recv(t_core, core_send.at[0], core_recv.at[0], core)
    t_pair[...] = t_own[...] + t_core[...]
    t_z[z] = t_pair[...]
    for j, p in enumerate(zs_of):
        send(t_pair, t_z.at[z], z_send.at[0, j], z_recv.at[0, z], z_dev[j])

    scores = mul(read, write, NT)
    cum_t = jnp.transpose(jnp.concatenate(
        [cum, ll_ref[0], ll_ref[1], jnp.zeros((128 - 3 * H, T), F32)], axis=0))
    later = t_row >= t_col
    same = (t_row // BLOCK) == (t_col // BLOCK)
    lane = iota((T, 128), 1)
    left = lane < width

    def head_mix(h):
        logit = jnp.where(same, cum_t[:, H + h:H + h + 1], cum_t[:, 2 * H + h:2 * H + h + 1])
        power = cum_t[:, h:h + 1] - cum[h:h + 1, :] + logit
        return jnp.exp(jnp.where(later, power, FAR))

    def local_pair(pair):
        vals = v_ref[:, pair * 128:(pair + 1) * 128]
        zero = jnp.zeros_like(vals)
        blocks = jnp.concatenate(
            [jnp.where(left, vals, zero), jnp.where(left, zero, vals)], axis=0)
        kernels = []
        for h in (2 * pair, 2 * pair + 1):
            mix = head_mix(h)
            md[h] = mix
            kernels.append(mix * scores)
        ya[:, pair * 128:(pair + 1) * 128] = left_two(
            jnp.concatenate(kernels, axis=1), blocks)

    local_pair(0)

    recv(core_e, core_send.at[1], core_recv.at[1], core)
    upper_total = jnp.where(k == 1, t_own[...], t_core[...])
    upper_decay = wide(jnp.exp(upper_total))
    from_own = kf + (1.0 - kf) * upper_decay
    from_core = (1.0 - kf) + kf * upper_decay
    mine = rows(k * half, half)
    s1h[...] = own_e[mine, :] * from_own + core_e[mine, :] * from_core
    zr[z] = s1h[rows(z * SR, SR), :]
    for j, p in enumerate(zs_of):
        send(s1h.at[rows(p * SR, SR)], zr.at[z], z_send.at[1, j], z_recv.at[1, z], z_dev[j])

    for j, p in enumerate(zs_of):
        recv(t_z.at[p], z_send.at[0, j], z_recv.at[0, p], z_dev[j])
    tz = [[t_z[i] for i in range(Z)]]
    for i in range(lz):
        tz.append([tz[i][2 * n] + tz[i][2 * n + 1] for n in range(Z >> (i + 1))])
    t_plane[...] = tz[lz][0]
    t_x[x] = tz[lz][0]
    for j, p in enumerate(xs_of):
        send(t_plane, t_x.at[x], x_send.at[1, j], x_recv.at[1, x], x_dev[j])

    local_pair(1)

    for j, p in enumerate(zs_of):
        recv(zr.at[p], z_send.at[1, j], z_recv.at[1, p], z_dev[j])
    z_decay = [[wide(jnp.exp(tile)) for tile in level] for level in tz]
    z_nodes = [zr]
    base = 0
    for i in range(lz):
        here = z_nodes[i]
        count = Z >> (i + 1)
        there = zs.at[base:base + count]
        for n in range(count):
            there[n] = here[2 * n] * z_decay[i][2 * n + 1] + here[2 * n + 1]
        z_nodes.append(there)
        base += count

    plane = z_nodes[lz].at[0]
    xr[x] = plane[...]
    for j, p in enumerate(xs_of):
        send(plane, xr.at[x], x_send.at[2, j], x_recv.at[2, x], x_dev[j])

    def to_readers(slot, source_of):
        place = rows(k * half + z * SR, SR)
        for j, p in enumerate(zs_of):
            send(source_of(p), st.at[slot, place], down_send.at[slot, j],
                 down_recv.at[slot, z], z_dev[j], needs(p, slot))

        @pl.when(needs(z, slot))
        def _():
            st[slot, place, :] = source_of(z)[...]

    def below(nodes, i):
        return lambda p: nodes[i].at[jnp.maximum(p // 2**i - 1, 0)]

    for i in reversed(range(lz)):
        to_readers(i, below(z_nodes, i))

    local_pair(2)

    for j, p in enumerate(xs_of):
        recv(t_x.at[p], x_send.at[1, j], x_recv.at[1, p], x_dev[j])
    tx = [[t_x[i] for i in range(X)]]
    for i in range(lx):
        tx.append([tx[i][2 * n] + tx[i][2 * n + 1] for n in range(X >> (i + 1))])
    x_decay = [[wide(jnp.exp(tile)) for tile in level] for level in tx]
    for j, p in enumerate(xs_of):
        recv(xr.at[p], x_send.at[2, j], x_recv.at[2, p], x_dev[j])
    x_nodes = [xr]
    base = 0
    for i in range(lx):
        here = x_nodes[i]
        count = X >> (i + 1)
        there = xs.at[base:base + count]
        for n in range(count):
            there[n] = here[2 * n] * x_decay[i][2 * n + 1] + here[2 * n + 1]
        x_nodes.append(there)
        base += count
    for i in range(lx):
        to_readers(lz + i, lambda p, i=i: x_nodes[i].at[jnp.maximum(x // 2**i - 1, 0)])

    whole = x_nodes[lx][0] * final_scale
    slice_row = iota((SR, C), 0)
    tile_lane = iota((H, 128), 1)

    def narrow(index):
        line = jnp.sum(jnp.where(slice_row == index, whole, 0.0), axis=0, keepdims=True)
        masked = jnp.where(pick, line, 0.0)
        tile = masked[:, 0:128]
        for n in range(1, C // 128):
            tile = tile + masked[:, n * 128:(n + 1) * 128]
        return tile + pltpu.roll(tile, width, 1)

    fs_ref[...] = jnp.where(tile_lane < width, narrow(2 * x), narrow(2 * x + 1))

    offset = jnp.zeros((H, 128), F32)
    for depth in range(cross):
        wx[depth] = spread_out(jnp.exp(ll_ref[2 + depth] + (offset + cum)))
        if depth == 0:
            offset = offset + jnp.where(k == 1, t_core[...], 0.0)
        elif depth <= lz:
            i = depth - 1
            for n in range(0, Z >> i, 2):
                offset = offset + jnp.where(z // 2**i == n + 1, tz[i][n], 0.0)
        else:
            i = depth - 1 - lz
            for n in range(0, X >> i, 2):
                offset = offset + jnp.where(x // 2**i == n + 1, tx[i][n], 0.0)

    local_pair(3)

    def read_level(depth, state):
        weighted = wx[depth] * right_two(read_p, state[...])
        wp[depth] = weighted
        ya[...] = ya[...] + weighted

    @pl.when(k == 1)
    def _():
        read_level(0, core_e)

    for slot in range(slots):
        for j, p in enumerate(zs_of):
            recv(st.at[slot, rows(k * half + p * SR, SR)], down_send.at[slot, j],
                 down_recv.at[slot, p], z_dev[j], needs(z, slot))
        send(st.at[slot, mine], st.at[slot, mine], core_send.at[2 + slot],
             core_recv.at[2 + slot], core, needs(z, slot))
    other = rows((1 - k) * half, half)
    for slot in range(slots):
        recv(st.at[slot, other], core_send.at[2 + slot], core_recv.at[2 + slot], core,
             needs(z, slot))

        @pl.when(needs(z, slot))
        def _():
            read_level(1 + slot, st.at[slot])

    gate = g_ref[...].astype(F32)
    sigma = jax.nn.sigmoid(gate)
    silu = gate * sigma
    out = ya[...]
    gated = out * silu
    gain = gain_ref[...]
    scaled = ct_ref[...].astype(F32) * gain
    ones = jnp.ones((8, C), BF16)
    squares = right_two(ones, gated * gated, NT)
    inners = right_two(ones, scaled * gated, NT)
    n_own[...] = jnp.where(iota((8, T), 0) == 0, squares, inners)
    for j, p in enumerate(ys_of):
        send(n_own, n_y.at[y], y_send.at[0, j], y_recv.at[0, y], y_dev[j])
    sums = n_own[...]
    for j, p in enumerate(ys_of):
        recv(n_y.at[p], y_send.at[0, j], y_recv.at[0, p], y_dev[j])
        sums = sums + n_y[p]
    columns = jnp.transpose(jnp.concatenate([sums, jnp.zeros((120, T), F32)], axis=0))
    inverse = lax.rsqrt(columns[:, 0:1] / channels + EPSILON)
    inner = inverse * columns[:, 1:2]
    normed = gated * inverse
    mixed_ref[...] = (normed * gain).astype(BF16)
    grad_gated = inverse * (scaled - normed * (inner / channels))
    gg_ref[...] = (grad_gated * out * sigma * (1.0 + gate * (1.0 - sigma))).astype(BF16)
    grad_out = grad_gated * silu
    ya[...] = grad_out

    def state_grad(depth):
        dl[depth] = right_two(read_t, ya[...] * wx[depth])

    for slot in reversed(range(slots)):
        @pl.when(needs(z, slot))
        def _():
            state_grad(1 + slot)

        send(dl.at[1 + slot, other], dr.at[slot], core_send.at[2 + slots + slot],
             core_recv.at[2 + slots + slot], core, needs(z, slot))

    @pl.when(k == 1)
    def _():
        state_grad(0)

    send(dl.at[0], d0, core_send.at[2 + 2 * slots], core_recv.at[2 + 2 * slots], core, k == 1)

    for slot in reversed(range(slots)):
        recv(dr.at[slot], core_send.at[2 + slots + slot], core_recv.at[2 + slots + slot], core,
             needs(z, slot))

        @pl.when(needs(z, slot))
        def _():
            dh[slot] = dl[1 + slot, mine, :] + dr[slot]
            zb[z, slot] = dh[slot, rows(z * SR, SR), :]

        for j, p in enumerate(zs_of):
            send(dh.at[slot, rows(p * SR, SR)], zb.at[z, slot], up_send.at[slot, j],
                 up_recv.at[slot, z], z_dev[j], needs(z, slot))

    gsc[...] = jnp.zeros((T, T), F32)
    block_pick = jnp.where(
        iota((8, T), 0) == iota((8, T), 1) // BLOCK, 1.0, 0.0).astype(BF16)
    late = iota((1, T), 1) >= BLOCK

    def backward_pair(pair):
        cols = slice(pair * 128, (pair + 1) * 128)
        vals = v_ref[:, cols]
        grads = ya[:, cols]
        zero = jnp.zeros_like(grads)
        parts = [jnp.where(left, grads, zero), jnp.where(left, zero, grads)]
        kernels = []
        for h, part in zip((2 * pair, 2 * pair + 1), parts):
            mix = md[h]
            kernel = mix * scores
            kernels.append(kernel)
            pull = left_two(part, vals, NT)
            gsc[...] = gsc[...] + pull * mix
            pulled = pull * kernel
            sums = right_two(block_pick, pulled, NT)
            first, second = sums[0:1, :], sums[1:2, :]
            gl_ref[0, h:h + 1, :] = jnp.where(late, second, first)
            gl_ref[1, h:h + 1, :] = jnp.where(late, first, 0.0)
            gsm[h:h + 1, :] = first + second - jnp.sum(pulled, axis=0, keepdims=True)
        gvl[:, cols] = both(
            jnp.concatenate(kernels, axis=0), jnp.concatenate(parts, axis=0), TN)

    backward_pair(0)
    backward_pair(1)

    for i in range(lx):
        slot = lz + i
        for j, p in enumerate(zs_of):
            recv(zb.at[p, slot], up_send.at[slot, j], up_recv.at[slot, p], z_dev[j],
                 needs(p, slot))

        @pl.when(bit(x, i))
        def _():
            acc = zb[0, slot]
            for p in range(1, Z):
                acc = acc + zb[p, slot]
            xbs[i] = acc

        @pl.when(jnp.logical_not(bit(x, i)))
        def _():
            xbs[i] = jnp.zeros((SR, C), F32)

    for j, p in enumerate(xs_of):
        send(xbs, xb.at[x], x_send.at[3, j], x_recv.at[3, x], x_dev[j])

    backward_pair(2)
    backward_pair(3)

    part_r[...] = left_two(gsc[...], write_p)
    part_w[...] = left_two(gsc[...], read_p, TN)
    pulled_all = jnp.zeros((H, T), F32)

    def level_back(depth, state):
        weighted = ya[...] * wx[depth]
        part_r[...] = part_r[...] + both(weighted, state[...], NT)
        gl_ref[2 + depth] = right_two(pick16, ya[...] * wp[depth], NT)

    for depth in range(cross):
        cond = (k == 1) if depth == 0 else needs(z, depth - 1)

        @pl.when(cond)
        def _():
            level_back(depth, core_e if depth == 0 else st.at[depth - 1])

        @pl.when(jnp.logical_not(cond))
        def _():
            gl_ref[2 + depth] = jnp.zeros((H, T), F32)

    chunk = T // Y
    for j, p in enumerate(ys_of):
        send(part_r.at[rows(p * chunk, chunk)], rs_r.at[y], y_send.at[1, j], y_recv.at[1, y],
             y_dev[j])

    for j, p in enumerate(xs_of):
        recv(f_x.at[p], x_send.at[0, j], x_recv.at[0, p], x_dev[j])
    f_x[x] = f_own[...]
    grad = jnp.zeros((SR, C), F32)
    for n in range(X):
        tile = f_x[n]
        turned = pltpu.roll(tile, width, 1)
        grad = jnp.where(slice_row == 2 * n, wide(jnp.where(tile_lane < width, tile, turned)), grad)
        grad = jnp.where(
            slice_row == 2 * n + 1, wide(jnp.where(tile_lane < width, turned, tile)), grad)
    grad = grad * final_scale

    for j, p in enumerate(xs_of):
        recv(xb.at[p], x_send.at[3, j], x_recv.at[3, p], x_dev[j])
    xb[x] = xbs[...]
    for i in reversed(range(lx)):
        lower = grad
        for n in range(0, X >> i, 2):
            read_by = xb[(n + 1) << i, i]
            for m in range(1, 1 << i):
                read_by = read_by + xb[((n + 1) << i) + m, i]
            lower = jnp.where(x // 2**i == n, grad * x_decay[i][n + 1] + read_by, lower)
        grad = lower
    for slot in reversed(range(lz)):
        for j, p in enumerate(zs_of):
            recv(zb.at[p, slot], up_send.at[slot, j], up_recv.at[slot, p], z_dev[j],
                 needs(p, slot))
    grads = [grad]
    for i in reversed(range(lz)):
        deeper = []
        for n in range(Z >> i):
            above = grads[n // 2]
            if n % 2 == 0:
                above = above * z_decay[i][n + 1]
                for m in range(1 << i):
                    above = above + zb[((n + 1) << i) + m, i]
            deeper.append(above)
        grads = deeper
    for n in range(Z):
        g1s[n] = grads[n]
    place = rows(k * half + z * SR, SR)
    for j, p in enumerate(zs_of):
        send(g1s.at[p], g1.at[place], z_send.at[2, j], z_recv.at[2, z], z_dev[j])
    g1[place, :] = g1s[z]

    acc = part_r[rows(y * chunk, chunk), :]
    for j, p in enumerate(ys_of):
        recv(rs_r.at[p], y_send.at[1, j], y_recv.at[1, p], y_dev[j])
        acc = acc + rs_r[p]
    own_r[...] = exact(acc, order.astype(F32))
    for j, p in enumerate(ys_of):
        send(own_r, ag_r.at[y], y_send.at[2, j], y_recv.at[2, y], y_dev[j])
    ag_r[y] = own_r[...]

    for j, p in enumerate(zs_of):
        recv(g1.at[rows(k * half + p * SR, SR)], z_send.at[2, j], z_recv.at[2, p], z_dev[j])
    last = 3 + 2 * slots
    send(g1.at[mine], g1.at[mine], core_send.at[last], core_recv.at[last], core)
    recv(d0, core_send.at[last - 1], core_recv.at[last - 1], core, k == 0)
    recv(g1.at[other], core_send.at[last], core_recv.at[last], core)

    end_grad = g1[...] * from_own + d0[...]
    end_high, end_low = split(end_grad)
    spread = mul(write_p, end_high) + mul(write_p, end_low)
    faded = fd[...]
    faded_high, faded_low = split(faded)
    part_w[...] = part_w[...] + (
        mul(faded_high, end_high, NT)
        + (mul(faded_low, end_high, NT) + mul(faded_high, end_low, NT)))
    for j, p in enumerate(ys_of):
        send(part_w.at[rows(p * chunk, chunk)], rs_w.at[y], y_send.at[3, j], y_recv.at[3, y],
             y_dev[j])
    fade_pull = right_two(pick16, faded * spread, NT)
    pulled_all = gl_ref[2]
    for depth in range(1, cross):
        pulled_all = pulled_all + gl_ref[2 + depth]
    passing = jnp.sum(pulled_all, axis=1, keepdims=True)
    change = jnp.sum(fade_pull, axis=1, keepdims=True) - passing
    v_own[...] = jnp.broadcast_to(change, (H, 128))
    send(v_own, v_core, core_send.at[last + 1], core_recv.at[last + 1], core)
    gv_ref[...] = (gvl[...] + spread * fx[...]).astype(BF16)
    recv(v_core, core_send.at[last + 1], core_recv.at[last + 1], core)
    v_pair[...] = v_own[...] + v_core[...]
    for j, p in enumerate(zs_of):
        send(v_pair, v_z.at[z], z_send.at[3, j], z_recv.at[3, z], z_dev[j])

    acc = part_w[rows(y * chunk, chunk), :]
    for j, p in enumerate(ys_of):
        recv(rs_w.at[p], y_send.at[3, j], y_recv.at[3, p], y_dev[j])
        acc = acc + rs_w[p]
    own_w[...] = exact(acc, order.astype(F32))
    for j, p in enumerate(ys_of):
        send(own_w, ag_w.at[y], y_send.at[4, j], y_recv.at[4, y], y_dev[j])
    ag_w[y] = own_w[...]

    passed = jnp.where(k == 1, v_core[...], 0.0)
    for j, p in enumerate(zs_of):
        recv(v_z.at[p], z_send.at[3, j], z_recv.at[3, p], z_dev[j])
    v_z[z] = v_pair[...]
    in_plane = jnp.zeros((H, 128), F32)
    for p in range(Z):
        tile = v_z[p]
        in_plane = in_plane + tile
        passed = passed + jnp.where(z > p, tile, 0.0)
    v_plane[...] = in_plane
    for j, p in enumerate(xs_of):
        send(v_plane, v_x.at[x], x_send.at[4, j], x_recv.at[4, x], x_dev[j])
    within = exact(pulled_all + gsm[...], jnp.where(t_row >= t_col, 1.0, 0.0))
    within = within + exact(fade_pull, jnp.where(t_row < t_col, 1.0, 0.0)) - passing
    for j, p in enumerate(xs_of):
        recv(v_x.at[p], x_send.at[4, j], x_recv.at[4, p], x_dev[j])
    v_x[x] = in_plane
    for p in range(X):
        passed = passed + jnp.where(x > p, v_x[p], 0.0)
    gd_ref[...] = within + passed[:, 0:1]

    for j, p in enumerate(ys_of):
        recv(ag_r.at[p], y_send.at[2, j], y_recv.at[2, p], y_dev[j])
    for p in range(Y):
        gr_ref[p * chunk:(p + 1) * chunk, :] = ag_r[p]
    for j, p in enumerate(ys_of):
        recv(ag_w.at[p], y_send.at[4, j], y_recv.at[4, p], y_dev[j])
    for p in range(Y):
        gw_ref[p * chunk:(p + 1) * chunk, :] = ag_w[p]

    for item, cond in sent:
        if cond is None:
            item.wait_send()
        else:
            pl.when(cond)(item.wait_send)


def shards(X, Z, Y, values, gate, write, read, decay, logit, gain, cot, final_cot):
    T, C = values.shape
    N = write.shape[1]
    H = decay.shape[0]
    width = C // H
    SR = 2 * X
    half = Z * SR
    lz, lx = Z.bit_length() - 1, X.bit_length() - 1
    slots = lz + lx
    cross = 1 + slots
    chunk = T // Y

    def mem(*shape, dtype=F32):
        return pltpu.VMEM(shape, dtype)

    sem = pltpu.SemaphoreType.DMA
    scratch = dict(
        fx=mem(T, C), fd=mem(T, C), own_e=mem(N, C), core_e=mem(N, C),
        s1h=mem(half, C), zr=mem(Z, SR, C), zs=mem(Z - 1, SR, C),
        xr=mem(X, SR, C), xs=mem(X - 1, SR, C), st=mem(slots, N, C),
        wx=mem(cross, T, C), wp=mem(cross, T, C), md=mem(H, T, T), ya=mem(T, C),
        dl=mem(cross, N, C), dr=mem(slots, half, C), d0=mem(N, C), dh=mem(slots, half, C),
        zb=mem(Z, slots, SR, C), xbs=mem(lx, SR, C), xb=mem(X, lx, SR, C),
        g1s=mem(Z, SR, C), g1=mem(N, C), gsc=mem(T, T), gvl=mem(T, C), gsm=mem(H, T),
        t_own=mem(H, 128), t_core=mem(H, 128), t_pair=mem(H, 128), t_z=mem(Z, H, 128),
        t_plane=mem(H, 128), t_x=mem(X, H, 128), f_own=mem(H, 128), f_x=mem(X, H, 128),
        v_own=mem(H, 128), v_core=mem(H, 128), v_pair=mem(H, 128), v_z=mem(Z, H, 128),
        v_plane=mem(H, 128), v_x=mem(X, H, 128),
        n_own=mem(8, T), n_y=mem(Y, 8, T),
        part_r=mem(T, N), rs_r=mem(Y, chunk, N), ag_r=mem(Y, chunk, N), own_r=mem(chunk, N),
        part_w=mem(T, N), rs_w=mem(Y, chunk, N), ag_w=mem(Y, chunk, N), own_w=mem(chunk, N),
        core_send=sem((5 + 2 * slots,)), core_recv=sem((5 + 2 * slots,)),
        z_send=sem((4, Z)), z_recv=sem((4, Z)), x_send=sem((5, X)), x_recv=sem((5, X)),
        y_send=sem((5, Y)), y_recv=sem((5, Y)),
        down_send=sem((slots, Z)), down_recv=sem((slots, Z)),
        up_send=sem((slots, Z)), up_recv=sem((slots, Z)),
    )
    vmem = pl.BlockSpec(memory_space=pltpu.VMEM)
    return pl.pallas_call(
        functools.partial(layer, (X, Z, Y, T, N, H, width)),
        out_shape=(
            jax.ShapeDtypeStruct((T, C), BF16),
            jax.ShapeDtypeStruct((T, C), BF16),
            jax.ShapeDtypeStruct((T, C), BF16),
            jax.ShapeDtypeStruct((T, N), F32),
            jax.ShapeDtypeStruct((T, N), F32),
            jax.ShapeDtypeStruct((H, T), F32),
            jax.ShapeDtypeStruct(logit.shape, F32),
            jax.ShapeDtypeStruct(final_cot.shape, F32),
        ),
        in_specs=[vmem] * 9,
        out_specs=(vmem,) * 8,
        scratch_shapes=list(scratch.values()),
        compiler_params=pltpu.CompilerParams(
            collective_id=0, has_side_effects=True, vmem_limit_bytes=56 * 2**20
        ),
    )(values, gate, write, read, decay, logit, gain.reshape(1, C), cot, final_cot)


def solution(mesh):
    ctx, heads = mesh.shape["ctx"], mesh.shape["head"]
    X = 1 << ((ctx.bit_length() - 2) // 2)
    Z = ctx // 2 // X
    return jax.shard_map(
        functools.partial(shards, X, Z, heads),
        mesh=mesh,
        in_specs=(
            P("ctx", "head"),
            P("ctx", "head"),
            P("ctx", None),
            P("ctx", None),
            P("head", "ctx"),
            P(None, "head", "ctx"),
            P("head"),
            P("ctx", "head"),
            P("head", "ctx"),
        ),
        out_specs=(
            P("ctx", "head"),
            P("ctx", "head"),
            P("ctx", "head"),
            P("ctx", None),
            P("ctx", None),
            P("head", "ctx"),
            P(None, "head", "ctx"),
            P("head", "ctx"),
        ),
        check_vma=False,
    )
```

time: 449 us -> 89.9 us (0.20); the launches traced: 441 us -> 89.5 us
  starting transfers between devices: 122 us -> 0 us
  waiting for transfers between devices: 91.6 us -> 0 us
  Pallas kernels: 0 us -> 82 us
  local copies, waits for them, and re-layouts: 75.3 us -> 6.82 us
  matrix products: 66.3 us -> 0 us
  loops' own time: 31.9 us -> 0 us
  blocking collectives: 25.4 us -> 0 us
  between operations: 15.5 us -> 0.66 us
  other arithmetic: 13.1 us -> 0 us
    ppermute x24 -> x0, starting transfers between devices: 122 us -> none  [swapped(): lax.ppermute(shard, axis, [(i, i ^ 1 << apart) for i in range(lax.axis_si...]
    pallas_call x0 -> x1, Pallas kernels: none -> 82 us  [shards(): pl.pallas_call(functools.partial(layer, (X, Z, Y, T, N, H, width)), out_s...]
    dot_general x72 -> x0, matrix products: 66.3 us -> none  [the longest x16 28.3 us: head_scores(): jnp.einsum('lt,lts->ts', weights_all[:local_levels + 1, head], masks, pre...]
    ppermute x24 -> x0, waiting for transfers between devices: 49.2 us -> none  [swapped(): lax.ppermute(shard, axis, [(i, i ^ 1 << apart) for i in range(lax.axis_si...]
    psum x1 -> x0, waiting for transfers between devices: 42.5 us -> none  [shards(): grad_write, grad_read = lax.psum((grad_write, grad_read), 'head')]
    another operation x2 -> x0, loops' own time: 31.9 us -> none  [the longest x1 16 us: shards(): local_out = lax.map(local_forward, jnp.arange(heads))]
    psum x2 -> x0, blocking collectives: 25.4 us -> none  [the longest x1 13.9 us: shards(): square_sum = lax.psum(jnp.sum(gated * gated, axis=1), 'head')]
    dynamic_update_slice x16 -> x0, local copies, waits for them, and re-layouts: 21 us -> none  [shards(): lax.scan(local_backward, jnp.zeros((rows, rows), jnp.float32), jnp.arange...]
  transfers between devices with their start and end apart: 25 -> 0, of which waited for: 18 -> 0; matrix products, arithmetic and copies ran while one was open for 7% -> 0% of each run, Pallas kernels for 0% -> 0%
where the time goes in v1:
time: 89.9 us; the launch traced here: 89.5 us
  Pallas kernels  82 us (91%)
  local copies, waits for them, and re-layouts  6.82 us (8%)
    pallas_call x1, Pallas kernels, shards(): pl.pallas_call(functools.partial(layer, (X, Z, Y, T, N, H, width)), out_s...  82 us
    unnamed x22, local copies, waits for them, and re-layouts  6.82 us

profile of v1, /device:TPU:1, one launch (start us, length us, event | category | flops | bytes accessed | tf_op | source)
XLA Modules:
  0.0 89.5 jit_solution(17683577827369999692)
XLA Ops:
  0.6 82.0 %shard_map.152 = (bf16[128,512]{1,0:T(8,128)(2,1)}, bf16[128,512]{1,0:T(8,128)(2,1)}, bf16[128,512]{1,0:T(8,128)(2,1)}, f32[128,128]{1,0:T(8,128)}, f32[128,128]...) custom-call(bf16[128,512]{1,0:T(8,128)(2,1)} %v_ref.1, bf16[128,512]{1,0:T(8,128)(2,1)} %g_ref.1, ...), custom_call_target="tpu_custom_call" | custom-call | tf_op jit(solution)/shard_map/pallas_call | solution.py:653
  82.7 0.0 copy-start.1
  82.7 1.6 %copy.25 = bf16[128,512]{1,0:T(8,128)(2,1)} copy(bf16[128,512]{1,0:T(8,128)(2,1)} %get-tuple-element.16) | data formatting | bytes 262144
  84.3 0.0 copy-done.1
  84.3 0.0 copy-start
  84.3 0.7 copy.26
  85.0 0.3 copy-done
  85.2 0.0 copy-start.3
  85.3 0.7 copy.27
  85.9 0.2 copy-done.3
  86.1 0.0 copy-start.2
  86.1 0.6 copy.28
  86.7 0.2 copy-done.2
  87.0 0.0 copy-start.6
  87.0 0.0 copy-start.4
  87.0 0.6 copy.29
  87.6 0.0 copy-done.6
  87.6 0.6 copy.30
  88.2 0.0 copy-done.4
  88.2 0.0 copy-start.5
  88.2 0.6 copy.31
  88.9 0.1 copy-done.5
  88.9 0.6 copy.32
Async XLA Ops:
  82.7 1.6 %copy-start.1 = (bf16[128,512]{1,0:T(8,128)(2,1)S(1)}, bf16[128,512]{1,0:T(8,128)(2,1)}, u32[]{:S(2)}) copy-start(bf16[128,512]{1,0:T(8,128)(2,1)} %get-tuple-element.17) | copy-start | bytes 393220
  84.3 1.0 %copy-start = (bf16[128,512]{1,0:T(8,128)(2,1)S(1)}, bf16[128,512]{1,0:T(8,128)(2,1)}, u32[]{:S(2)}) copy-start(bf16[128,512]{1,0:T(8,128)(2,1)} %get-tuple-element.18) | copy-start | bytes 393220
  85.2 0.9 copy-start.3
  86.1 0.9 copy-start.2
  87.0 0.7 copy-start.6
  87.0 1.3 %copy-start.4 = (f32[8,8,128]{2,1,0:T(8,128)S(1)}, f32[8,8,128]{2,1,0:T(8,128)}, u32[]{:S(2)}) copy-start(f32[8,8,128]{2,1,0:T(8,128)} %get-tuple-element.22) | copy-start | bytes 98308
  88.2 0.7 copy-start.5

commit v2 on v1

v2 whole, which is shorter than its diff:
```python
import functools

import jax
import jax.numpy as jnp
from jax import lax
from jax.experimental import pallas as pl
from jax.experimental.pallas import tpu as pltpu
from jax.sharding import PartitionSpec as P

F32 = jnp.float32
BF16 = jnp.bfloat16
EPSILON = 1e-05
BLOCK = 64
FAR = -1e30
NN = (((1,), (0,)), ((), ()))
NT = (((1,), (1,)), ((), ()))
TN = (((0,), (0,)), ((), ()))


def split(array):
    high = array.astype(BF16)
    return high, (array - high.astype(F32)).astype(BF16)


def mul(a, b, dims=NN):
    return lax.dot_general(a, b, dims, preferred_element_type=F32)


def left_two(a, b, dims=NN):
    high, low = split(a)
    return mul(high, b, dims) + mul(low, b, dims)


def right_two(a, b, dims=NN):
    high, low = split(b)
    return mul(a, high, dims) + mul(a, low, dims)


def both(a, b, dims=NN):
    a_high, a_low = split(a)
    b_high, b_low = split(b)
    return mul(a_high, b_high, dims) + (mul(a_low, b_high, dims) + mul(a_high, b_low, dims))


def exact(a, b, dims=NN):
    return lax.dot_general(
        a, b, dims, precision=lax.Precision.HIGHEST, preferred_element_type=F32
    )


def left_three(a, b, dims=NN):
    high = a.astype(BF16)
    rest = a - high.astype(F32)
    middle, low = split(rest)
    return mul(high, b, dims) + (mul(middle, b, dims) + mul(low, b, dims))


def iota(shape, dim):
    return lax.broadcasted_iota(jnp.int32, shape, dim)


def far_first(count):
    return sorted(range(1, count), key=lambda j: -min(j, count - j))


def layer(
    sizes,
    v_ref, g_ref, b_ref, r_ref, ld_ref, ll_ref, gain_ref, ct_ref, fc_ref,
    mixed_ref, gv_ref, gg_ref, gw_ref, gr_ref, gd_ref, gl_ref, fs_ref,
    fx, fd, fh, fl, silu_, slope, own_e, core_e, s1h, zr, zs, xr, xs, st,
    wx, wp, md, ya, dl, dr, d0, dh, zb, d1, xbs, xb, gp, g1s, g1, gsc, gvl, gsm,
    t_own, t_core, t_pair, t_z, t_plane, t_x, f_own, f_x,
    v_own, v_core, v_pair, v_z, v_plane, v_x,
    n_own, n_y, part_r, rs_r, ag_r, own_r, part_w, rs_w, ag_w, own_w,
    core_send, core_recv, z_send, z_recv, x_send, x_recv, y_send, y_recv,
    down_send, down_recv, up_send, up_recv, pair_send, pair_recv,
):
    X, Z, Y, T, N, H, width = sizes
    C = H * width
    SR = 2 * X
    half = Z * SR
    lz, lx = Z.bit_length() - 1, X.bit_length() - 1
    cross = 1 + lz + lx
    slots = lz + lx
    final_scale = (N / (T * X * Z * 2)) ** 0.5
    channels = C * Y

    me = lax.axis_index("ctx")
    y = lax.axis_index("head")
    k = me % 2
    z = (me // 2) % Z
    x = me // (2 * Z)
    kf = k.astype(F32)

    def device(x_, z_, k_, y_):
        return (x_ * (2 * Z) + z_ * 2 + k_, y_)

    core_links = (core_send, core_recv, k, [(1 - k, device(x, z, 1 - k, y))])
    z_links = (z_send, z_recv, z, [
        (p, device(x, p, k, y)) for p in [(z + j) % Z for j in far_first(Z)]])
    down_links = (down_send, down_recv) + z_links[2:]
    up_links = (up_send, up_recv) + z_links[2:]
    x_links = (x_send, x_recv, x, [
        (p, device(p, z, k, y)) for p in [(x + j) % X for j in far_first(X)]])
    y_links = (y_send, y_recv, y, [
        (p, device(x, z, k, p)) for p in [(y + j) % Y for j in far_first(Y)]])
    z_pair = z + 1 - 2 * (z % 2)
    pair_links = (pair_send, pair_recv, 0, [(0, device(x, z_pair, k, y))])
    all_z = [(z + j) % Z for j in far_first(Z) + [0]]

    def plane_links(sends, recvs, plane):
        return (sends, recvs, z, [(p, device(plane, p, k, y)) for p in all_z])

    next_plane = x + 1 - 2 * (x % 2)
    mirror_plane = X - 1 - x

    barrier = pltpu.get_barrier_semaphore()
    peers = [dev for links in (core_links, z_links, x_links, y_links) for _, dev in links[3]]
    peers += [device(next_plane, p, k, y) for p in all_z[:-1]]
    if lx > 1:
        peers += [device(mirror_plane, p, k, y) for p in all_z[:-1]]
    for peer in peers:
        pl.semaphore_signal(barrier, inc=1, device_id=peer, device_id_type=pl.DeviceIdType.MESH)

    sent = []

    def do(cond, action):
        if cond is None:
            action()
        else:
            pl.when(cond)(action)

    def exchange(links, slot, src_of, dst_of, send_if=lambda p: None, recv_if=lambda p: None):
        send_sems, recv_sems, mine_, others = links

        def item(n, src, dst, sender):
            return pltpu.make_async_remote_copy(
                src_ref=src, dst_ref=dst, send_sem=send_sems.at[slot, n],
                recv_sem=recv_sems.at[slot, sender], device_id=others[n][1],
                device_id_type=pl.DeviceIdType.MESH,
            )

        for n, (p, _) in enumerate(others):
            out = item(n, src_of(p), dst_of(mine_), mine_)
            do(send_if(p), out.start)
            sent.append((send_if(p), out.wait_send))

        def wait():
            for n, (p, _) in enumerate(others):
                do(recv_if(p), item(n, dst_of(p), dst_of(p), p).wait_recv)

        return wait

    def bit(index, place):
        return (index // 2**place) % 2 == 1

    def needs(z_, slot):
        return bit(z_, slot) if slot < lz else bit(x, slot - lz)

    def rows(start, size):
        return pl.ds(pl.multiple_of(start, size), size)

    head_of = iota((H, C), 1) // width
    pick = head_of == iota((H, C), 0)
    pick16 = jnp.where(pick, 1.0, 0.0).astype(BF16)

    def wide(tile):
        many = jnp.concatenate([tile] * (C // 128), axis=1)
        return jnp.sum(jnp.where(pick, many, 0.0), axis=0, keepdims=True)

    def spread_out(array):
        return left_two(array, pick16, TN)

    j_ = iota((N, N), 0)
    n_ = iota((N, N), 1)
    natural = ((j_ % SR) // 2) * (4 * Z) + ((j_ % half) // SR) * 4 + (j_ // half) * 2 + j_ % 2
    order = jnp.where(natural == n_, 1.0, 0.0).astype(BF16)

    write = b_ref[...]
    read = r_ref[...]
    write_p = mul(write, order, NT).astype(BF16)
    write_t = mul(order, write, NT).astype(BF16)
    read_p = mul(read, order, NT).astype(BF16)
    read_t = mul(order, read, NT).astype(BF16)

    t_row = iota((T, T), 0)
    t_col = iota((T, T), 1)
    upto = jnp.where(t_row <= t_col, 1.0, 0.0)
    cum = exact(ld_ref[...], upto)
    total = jnp.broadcast_to(cum[:, T - 1:T], (H, 128))
    t_own[...] = total
    fade = jnp.exp(cum[:, T - 1:T] - cum)
    fx[...] = spread_out(fade)
    faded = v_ref[...].astype(F32) * fx[...]
    fd[...] = faded
    own_e[...] = right_two(write_t, faded)
    f_own[...] = fc_ref[...]

    @pl.when(k == 1)
    def _():
        d0[...] = jnp.zeros((N, C), F32)

    pl.semaphore_wait(barrier, len(peers))

    wait_total = exchange(core_links, 0, lambda p: t_own, lambda p: t_core)
    wait_end = exchange(core_links, 1, lambda p: own_e, lambda p: core_e)
    wait_final = exchange(x_links, 0, lambda p: f_own, lambda p: f_x.at[p])

    wait_total()
    t_pair[...] = t_own[...] + t_core[...]
    t_z[z] = t_pair[...]
    wait_pairs = exchange(z_links, 0, lambda p: t_pair, lambda p: t_z.at[p])

    wait_end()
    upper_total = jnp.where(k == 1, t_own[...], t_core[...])
    upper_decay = wide(jnp.exp(upper_total))
    from_own = kf + (1.0 - kf) * upper_decay
    from_core = (1.0 - kf) + kf * upper_decay
    mine = rows(k * half, half)
    s1h[...] = own_e[mine, :] * from_own + core_e[mine, :] * from_core
    wait_slices = exchange(z_links, 1, lambda p: s1h.at[rows(p * SR, SR)], lambda p: zr.at[p])
    wait_state = [None] * slots
    wait_half = [None] * slots
    wait_state[0] = exchange(
        pair_links, 0, lambda p: s1h, lambda p: st.at[0, mine],
        lambda p: z % 2 == 0, lambda p: z % 2 == 1)
    zr[z] = s1h[rows(z * SR, SR), :]

    scores = mul(read, write, NT)
    cum_t = jnp.transpose(jnp.concatenate(
        [cum, ll_ref[0], ll_ref[1], jnp.zeros((128 - 3 * H, T), F32)], axis=0))
    later = t_row >= t_col
    same = (t_row // BLOCK) == (t_col // BLOCK)
    lane = iota((T, 128), 1)
    left = lane < width

    def head_mix(h):
        logit = jnp.where(same, cum_t[:, H + h:H + h + 1], cum_t[:, 2 * H + h:2 * H + h + 1])
        power = cum_t[:, h:h + 1] - cum[h:h + 1, :] + logit
        return jnp.exp(jnp.where(later, power, FAR))

    def local_pair(pair):
        vals = v_ref[:, pair * 128:(pair + 1) * 128]
        zero = jnp.zeros_like(vals)
        blocks = jnp.concatenate(
            [jnp.where(left, vals, zero), jnp.where(left, zero, vals)], axis=0)
        kernels = []
        for h in (2 * pair, 2 * pair + 1):
            mix = head_mix(h)
            md[h] = mix
            kernels.append(mix * scores)
        ya[:, pair * 128:(pair + 1) * 128] = left_two(
            jnp.concatenate(kernels, axis=1), blocks)

    local_pair(0)

    wait_pairs()
    tz = [[t_z[i] for i in range(Z)]]
    for i in range(lz):
        tz.append([tz[i][2 * n] + tz[i][2 * n + 1] for n in range(Z >> (i + 1))])
    t_plane[...] = tz[lz][0]
    t_x[x] = tz[lz][0]
    wait_plane_totals = exchange(x_links, 1, lambda p: t_plane, lambda p: t_x.at[p])
    z_decay = [[wide(jnp.exp(tile)) for tile in level] for level in tz]

    local_pair(1)

    wait_slices()
    z_nodes = [zr]
    base = 0
    for i in range(lz):
        here = z_nodes[i]
        count = Z >> (i + 1)
        there = zs.at[base:base + count]
        for n in range(count):
            there[n] = here[2 * n] * z_decay[i][2 * n + 1] + here[2 * n + 1]
        z_nodes.append(there)
        base += count

    plane = z_nodes[lz].at[0]
    xr[x] = plane[...]
    wait_planes = exchange(x_links, 2, lambda p: plane, lambda p: xr.at[p])

    def slice_of(slot):
        return lambda p: st.at[slot, rows(k * half + p * SR, SR)]

    wait_state[lz] = exchange(
        plane_links(down_send, down_recv, next_plane), lz, lambda p: plane, slice_of(lz),
        lambda p: x % 2 == 0, lambda p: x % 2 == 1)
    for i in reversed(range(1, lz)):
        def below(p, i=i):
            return z_nodes[i].at[jnp.maximum(p // 2**i - 1, 0)]

        wait_state[i] = exchange(
            down_links, i, below, slice_of(i), lambda p, i=i: bit(p, i),
            lambda p, i=i: bit(z, i))

        @pl.when(bit(z, i))
        def _():
            st[i, rows(k * half + z * SR, SR), :] = below(z)[...]

    def from_core_too(slot):
        wait_state[slot]()
        wait_half[slot] = exchange(
            core_links, 2 + slot, lambda p: st.at[slot, mine],
            lambda p: st.at[slot, rows(p * half, half)],
            lambda p: needs(z, slot), lambda p: needs(z, slot))

    local_pair(2)
    from_core_too(0)

    wait_plane_totals()
    tx = [[t_x[i] for i in range(X)]]
    for i in range(lx):
        tx.append([tx[i][2 * n] + tx[i][2 * n + 1] for n in range(X >> (i + 1))])
    x_decay = [[wide(jnp.exp(tile)) for tile in level] for level in tx]
    wait_planes()
    x_nodes = [xr]
    base = 0
    for i in range(lx):
        here = x_nodes[i]
        count = X >> (i + 1)
        there = xs.at[base:base + count]
        for n in range(count):
            there[n] = here[2 * n] * x_decay[i][2 * n + 1] + here[2 * n + 1]
        x_nodes.append(there)
        base += count
    if lx > 1:
        lower = x_nodes[1].at[0]
        wait_cross = exchange(
            plane_links(down_send, down_recv, mirror_plane), lz + 1, lambda p: lower,
            slice_of(lz + 1), lambda p: x == 1, lambda p: x == 2)
        wait_inside = exchange(
            down_links, lz + 2, lambda p: lower, slice_of(lz + 1),
            lambda p: x == 3, lambda p: x == 3)

        @pl.when(x == 3)
        def _():
            st[lz + 1, rows(k * half + z * SR, SR), :] = lower[...]

        def wait_both():
            wait_cross()
            wait_inside()

        wait_state[lz + 1] = wait_both

    local_pair(3)

    offset = jnp.zeros((H, 128), F32)
    for depth in range(cross):
        wx[depth] = spread_out(jnp.exp(ll_ref[2 + depth] + (offset + cum)))
        if depth == 0:
            offset = offset + jnp.where(k == 1, t_core[...], 0.0)
        elif depth <= lz:
            i = depth - 1
            for n in range(0, Z >> i, 2):
                offset = offset + jnp.where(z // 2**i == n + 1, tz[i][n], 0.0)
        else:
            i = depth - 1 - lz
            for n in range(0, X >> i, 2):
                offset = offset + jnp.where(x // 2**i == n + 1, tx[i][n], 0.0)

    def read_level(depth, state):
        weighted = wx[depth] * right_two(read_p, state[...])
        wp[depth] = weighted
        ya[...] = ya[...] + weighted

    def read_slot(slot):
        wait_half[slot]()

        @pl.when(needs(z, slot))
        def _():
            read_level(1 + slot, st.at[slot])

    @pl.when(k == 1)
    def _():
        read_level(0, core_e)

    read_slot(0)

    whole = x_nodes[lx][0] * final_scale
    slice_row = iota((SR, C), 0)
    tile_lane = iota((H, 128), 1)

    def narrow(index):
        line = jnp.sum(jnp.where(slice_row == index, whole, 0.0), axis=0, keepdims=True)
        masked = jnp.where(pick, line, 0.0)
        tile = masked[:, 0:128]
        for n in range(1, C // 128):
            tile = tile + masked[:, n * 128:(n + 1) * 128]
        return tile + pltpu.roll(tile, width, 1)

    fs_ref[...] = jnp.where(tile_lane < width, narrow(2 * x), narrow(2 * x + 1))

    gate = g_ref[...].astype(F32)
    sigma = jax.nn.sigmoid(gate)
    silu_[...] = gate * sigma
    slope[...] = sigma * (1.0 + gate * (1.0 - sigma))
    faded_high, faded_low = split(fd[...])
    fh[...] = faded_high
    fl[...] = faded_low

    for slot in list(range(lz - 1, 0, -1)) + list(range(lz, slots)):
        from_core_too(slot)
        if slot < lz:
            read_slot(slot)
    for slot in range(lz, slots):
        read_slot(slot)

    silu = silu_[...]
    out = ya[...]
    gated = out * silu
    gain = gain_ref[...]
    scaled = ct_ref[...].astype(F32) * gain
    ones = jnp.ones((8, C), BF16)
    squares = right_two(ones, gated * gated, NT)
    inners = right_two(ones, scaled * gated, NT)
    n_own[...] = jnp.where(iota((8, T), 0) == 0, squares, inners)
    wait_norm = exchange(y_links, 0, lambda p: n_own, lambda p: n_y.at[p])
    wait_norm()
    n_y[y] = n_own[...]
    sums = n_y[0]
    for p in range(1, Y):
        sums = sums + n_y[p]
    columns = jnp.transpose(jnp.concatenate([sums, jnp.zeros((120, T), F32)], axis=0))
    inverse = lax.rsqrt(columns[:, 0:1] / channels + EPSILON)
    inner = inverse * columns[:, 1:2]
    normed = gated * inverse
    mixed_ref[...] = (normed * gain).astype(BF16)
    grad_gated = inverse * (scaled - normed * (inner / channels))
    gg_ref[...] = (grad_gated * out * slope[...]).astype(BF16)
    grad_out = grad_gated * silu
    ya[...] = grad_out

    def state_grad(depth):
        dl[depth] = right_two(read_t, ya[...] * wx[depth])

    wait_core_grad = [None] * slots
    wait_grad = [None] * slots
    other = rows((1 - k) * half, half)

    def start_slot(slot):
        @pl.when(needs(z, slot))
        def _():
            state_grad(1 + slot)

        wait_core_grad[slot] = exchange(
            core_links, 2 + slots + slot, lambda p: dl.at[1 + slot, rows(p * half, half)],
            lambda p: dr.at[slot], lambda p: needs(z, slot), lambda p: needs(z, slot))

    def finish_slot(slot):
        wait_core_grad[slot]()

        @pl.when(needs(z, slot))
        def _():
            dh[slot] = dl[1 + slot, mine, :] + dr[slot]

        def piece(p):
            return dh.at[slot, rows(p * SR, SR)]

        if slot == 0:
            wait_grad[0] = exchange(
                pair_links, 1, lambda p: dh.at[0], lambda p: d1,
                lambda p: z % 2 == 1, lambda p: z % 2 == 0)
        elif slot == lz:
            wait_grad[slot] = exchange(
                plane_links(up_send, up_recv, next_plane), slot, piece, lambda p: zb.at[p, slot],
                lambda p: x % 2 == 1, lambda p: x % 2 == 0)
        else:
            wait_grad[slot] = exchange(
                up_links, slot, piece, lambda p: zb.at[p, slot],
                lambda p: needs(z, slot), lambda p: needs(p, slot))

            @pl.when(needs(z, slot))
            def _():
                zb[z, slot] = piece(z)[...]

    for slot in reversed(range(slots)):
        start_slot(slot)
        if slot + 1 < slots:
            finish_slot(slot + 1)

    @pl.when(k == 1)
    def _():
        state_grad(0)

    finish_slot(0)
    wait_lowest = exchange(
        core_links, 2 + 2 * slots, lambda p: dl.at[0], lambda p: d0,
        lambda p: k == 1, lambda p: k == 0)

    gsc[...] = jnp.zeros((T, T), F32)
    block_pick = jnp.where(
        iota((8, T), 0) == iota((8, T), 1) // BLOCK, 1.0, 0.0).astype(BF16)
    late = iota((1, T), 1) >= BLOCK

    def backward_pair(pair):
        cols = slice(pair * 128, (pair + 1) * 128)
        vals = v_ref[:, cols]
        grads = ya[:, cols]
        zero = jnp.zeros_like(grads)
        parts = [jnp.where(left, grads, zero), jnp.where(left, zero, grads)]
        kernels = []
        for h, part in zip((2 * pair, 2 * pair + 1), parts):
            mix = md[h]
            kernel = mix * scores
            kernels.append(kernel)
            pull = left_two(part, vals, NT)
            gsc[...] = gsc[...] + pull * mix
            pulled = pull * kernel
            sums = right_two(block_pick, pulled, NT)
            first, second = sums[0:1, :], sums[1:2, :]
            gl_ref[0, h:h + 1, :] = jnp.where(late, second, first)
            gl_ref[1, h:h + 1, :] = jnp.where(late, first, 0.0)
            gsm[h:h + 1, :] = first + second - jnp.sum(pulled, axis=0, keepdims=True)
        gvl[:, cols] = both(
            jnp.concatenate(kernels, axis=0), jnp.concatenate(parts, axis=0), TN)

    backward_pair(0)
    backward_pair(1)

    if lx > 1:
        wait_grad[lz + 1]()

        @pl.when(x >= 2)
        def _():
            acc = zb[0, lz + 1]
            for p in range(1, Z):
                acc = acc + zb[p, lz + 1]
            xbs[...] = acc

        wait_plane_grads = exchange(
            x_links, 3, lambda p: xbs, lambda p: xb.at[p],
            lambda p: jnp.logical_and(x >= 2, p < 2), lambda p: jnp.logical_and(x < 2, p >= 2))

    backward_pair(2)
    backward_pair(3)

    part_r[...] = left_two(gsc[...], write_p)
    part_w[...] = left_two(gsc[...], read_p, TN)
    pulled_all = jnp.zeros((H, T), F32)

    def level_back(depth, state):
        weighted = ya[...] * wx[depth]
        part_r[...] = part_r[...] + both(weighted, state[...], NT)
        gl_ref[2 + depth] = right_two(pick16, ya[...] * wp[depth], NT)

    for depth in range(cross):
        cond = (k == 1) if depth == 0 else needs(z, depth - 1)

        @pl.when(cond)
        def _():
            level_back(depth, core_e if depth == 0 else st.at[depth - 1])

        @pl.when(jnp.logical_not(cond))
        def _():
            gl_ref[2 + depth] = jnp.zeros((H, T), F32)

    chunk = T // Y
    wait_read_parts = exchange(
        y_links, 1, lambda p: part_r.at[rows(p * chunk, chunk)], lambda p: rs_r.at[p])

    wait_final()
    f_x[x] = f_own[...]
    grad = jnp.zeros((SR, C), F32)
    for n in range(X):
        tile = f_x[n]
        turned = pltpu.roll(tile, width, 1)
        grad = jnp.where(slice_row == 2 * n, wide(jnp.where(tile_lane < width, tile, turned)), grad)
        grad = jnp.where(
            slice_row == 2 * n + 1, wide(jnp.where(tile_lane < width, turned, tile)), grad)
    grad = grad * final_scale

    gp[...] = grad
    if lx > 1:
        wait_plane_grads()

        @pl.when(x < 2)
        def _():
            gp[...] = gp[...] * x_decay[1][1] + (xb[2] + xb[3])

    wait_grad[lz]()

    @pl.when(x % 2 == 0)
    def _():
        upper = tx[0][1]
        for n in range(3, X, 2):
            upper = jnp.where(x == n - 1, tx[0][n], upper)
        acc = zb[0, lz]
        for p in range(1, Z):
            acc = acc + zb[p, lz]
        gp[...] = gp[...] * wide(jnp.exp(upper)) + acc

    grad = gp[...]
    for slot in reversed(range(1, lz)):
        wait_grad[slot]()
    grads = [grad]
    for i in reversed(range(lz)):
        deeper = []
        for n in range(Z >> i):
            above = grads[n // 2]
            if n % 2 == 0:
                above = above * z_decay[i][n + 1]
                for m in range(1 << i if i else 0):
                    above = above + zb[((n + 1) << i) + m, i]
            deeper.append(above)
        grads = deeper
    for n in range(Z):
        g1s[n] = grads[n]
    wait_own_grad = exchange(
        z_links, 2, lambda p: g1s.at[p], lambda p: g1.at[rows(k * half + p * SR, SR)])
    g1[rows(k * half + z * SR, SR), :] = g1s[z]

    def own_chunk(part, received, own):
        received[y] = part[rows(y * chunk, chunk), :]
        acc = received[0]
        for p in range(1, Y):
            acc = acc + received[p]
        own[...] = left_three(acc, order)

    wait_read_parts()
    own_chunk(part_r, rs_r, own_r)
    wait_read = exchange(y_links, 2, lambda p: own_r, lambda p: ag_r.at[p])
    ag_r[y] = own_r[...]

    wait_own_grad()
    wait_grad[0]()

    @pl.when(z % 2 == 0)
    def _():
        g1[mine, :] = g1[mine, :] + d1[...]

    last = 3 + 2 * slots
    wait_half_grad = exchange(
        core_links, last, lambda p: g1.at[mine], lambda p: g1.at[rows(p * half, half)])
    wait_lowest()
    wait_half_grad()

    end_grad = g1[...] * from_own + d0[...]
    end_high, end_low = split(end_grad)
    part_w[...] = part_w[...] + (
        mul(fh[...], end_high, NT) + (mul(fl[...], end_high, NT) + mul(fh[...], end_low, NT)))
    wait_write_parts = exchange(
        y_links, 3, lambda p: part_w.at[rows(p * chunk, chunk)], lambda p: rs_w.at[p])
    spread = mul(write_p, end_high) + mul(write_p, end_low)
    fade_pull = right_two(pick16, fd[...] * spread, NT)
    pulled_all = gl_ref[2]
    for depth in range(1, cross):
        pulled_all = pulled_all + gl_ref[2 + depth]
    passing = jnp.sum(pulled_all, axis=1, keepdims=True)
    change = jnp.sum(fade_pull, axis=1, keepdims=True) - passing
    v_own[...] = jnp.broadcast_to(change, (H, 128))
    wait_change = exchange(core_links, last + 1, lambda p: v_own, lambda p: v_core)
    gv_ref[...] = (gvl[...] + spread * fx[...]).astype(BF16)
    wait_change()
    v_pair[...] = v_own[...] + v_core[...]
    wait_changes = exchange(z_links, 3, lambda p: v_pair, lambda p: v_z.at[p])

    wait_write_parts()
    own_chunk(part_w, rs_w, own_w)
    wait_write = exchange(y_links, 4, lambda p: own_w, lambda p: ag_w.at[p])
    ag_w[y] = own_w[...]

    passed = jnp.where(k == 1, v_core[...], 0.0)
    wait_changes()
    v_z[z] = v_pair[...]
    in_plane = jnp.zeros((H, 128), F32)
    for p in range(Z):
        tile = v_z[p]
        in_plane = in_plane + tile
        passed = passed + jnp.where(z > p, tile, 0.0)
    v_plane[...] = in_plane
    wait_plane_changes = exchange(x_links, 4, lambda p: v_plane, lambda p: v_x.at[p])
    within = exact(pulled_all + gsm[...], jnp.where(t_row >= t_col, 1.0, 0.0))
    within = within + exact(fade_pull, jnp.where(t_row < t_col, 1.0, 0.0)) - passing
    wait_plane_changes()
    v_x[x] = in_plane
    for p in range(X):
        passed = passed + jnp.where(x > p, v_x[p], 0.0)
    gd_ref[...] = within + passed[:, 0:1]

    wait_read()
    for p in range(Y):
        gr_ref[p * chunk:(p + 1) * chunk, :] = ag_r[p]
    wait_write()
    for p in range(Y):
        gw_ref[p * chunk:(p + 1) * chunk, :] = ag_w[p]

    for cond, wait_send in sent:
        do(cond, wait_send)


def copy_out(count, *refs):
    sems = refs[2 * count]
    copies = [
        pltpu.make_async_copy(refs[n], refs[count + n], sems.at[n]) for n in range(count)
    ]
    for item in copies:
        item.start()
    for item in copies:
        item.wait()


def shards(X, Z, Y, values, gate, write, read, decay, logit, gain, cot, final_cot):
    T, C = values.shape
    N = write.shape[1]
    H = decay.shape[0]
    width = C // H
    SR = 2 * X
    half = Z * SR
    lz, lx = Z.bit_length() - 1, X.bit_length() - 1
    slots = lz + lx
    cross = 1 + slots
    chunk = T // Y

    def mem(*shape, dtype=F32):
        return pltpu.VMEM(shape, dtype)

    sem = pltpu.SemaphoreType.DMA
    scratch = dict(
        fx=mem(T, C), fd=mem(T, C), fh=mem(T, C, dtype=BF16), fl=mem(T, C, dtype=BF16),
        silu_=mem(T, C), slope=mem(T, C), own_e=mem(N, C), core_e=mem(N, C),
        s1h=mem(half, C), zr=mem(Z, SR, C), zs=mem(Z - 1, SR, C),
        xr=mem(X, SR, C), xs=mem(X - 1, SR, C), st=mem(slots, N, C),
        wx=mem(cross, T, C), wp=mem(cross, T, C), md=mem(H, T, T), ya=mem(T, C),
        dl=mem(cross, N, C), dr=mem(slots, half, C), d0=mem(N, C), dh=mem(slots, half, C),
        zb=mem(Z, slots, SR, C), d1=mem(half, C), xbs=mem(SR, C), xb=mem(X, SR, C),
        gp=mem(SR, C), g1s=mem(Z, SR, C), g1=mem(N, C), gsc=mem(T, T), gvl=mem(T, C), gsm=mem(H, T),
        t_own=mem(H, 128), t_core=mem(H, 128), t_pair=mem(H, 128), t_z=mem(Z, H, 128),
        t_plane=mem(H, 128), t_x=mem(X, H, 128), f_own=mem(H, 128), f_x=mem(X, H, 128),
        v_own=mem(H, 128), v_core=mem(H, 128), v_pair=mem(H, 128), v_z=mem(Z, H, 128),
        v_plane=mem(H, 128), v_x=mem(X, H, 128),
        n_own=mem(8, T), n_y=mem(Y, 8, T),
        part_r=mem(T, N), rs_r=mem(Y, chunk, N), ag_r=mem(Y, chunk, N), own_r=mem(chunk, N),
        part_w=mem(T, N), rs_w=mem(Y, chunk, N), ag_w=mem(Y, chunk, N), own_w=mem(chunk, N),
        core_send=sem((5 + 2 * slots, 1)), core_recv=sem((5 + 2 * slots, 2)),
        z_send=sem((4, Z)), z_recv=sem((4, Z)), x_send=sem((5, X)), x_recv=sem((5, X)),
        y_send=sem((5, Y)), y_recv=sem((5, Y)),
        down_send=sem((slots + 1, Z)), down_recv=sem((slots + 1, Z)),
        up_send=sem((slots, Z)), up_recv=sem((slots, Z)),
        pair_send=sem((2, 1)), pair_recv=sem((2, 1)),
    )
    vmem = pl.BlockSpec(memory_space=pltpu.VMEM)
    outs = (
        ((T, C), BF16), ((T, C), BF16), ((T, C), BF16), ((T, N), F32), ((T, N), F32),
        ((H, T), F32), (logit.shape, F32), (final_cot.shape, F32),
    )
    results = pl.pallas_call(
        functools.partial(layer, (X, Z, Y, T, N, H, width)),
        out_shape=tuple(jax.ShapeDtypeStruct(shape, dtype) for shape, dtype in outs),
        in_specs=[vmem] * 9,
        out_specs=(vmem,) * 8,
        scratch_shapes=list(scratch.values()),
        compiler_params=pltpu.CompilerParams(
            collective_id=0, has_side_effects=True, vmem_limit_bytes=56 * 2**20
        ),
    )(values, gate, write, read, decay, logit, gain.reshape(1, C), cot, final_cot)
    anywhere = pl.BlockSpec(memory_space=pl.ANY)
    return pl.pallas_call(
        functools.partial(copy_out, len(results)),
        out_shape=tuple(jax.ShapeDtypeStruct(shape, dtype) for shape, dtype in outs),
        in_specs=[vmem] * len(results),
        out_specs=(anywhere,) * len(results),
        scratch_shapes=[sem((len(results),))],
    )(*results)


def solution(mesh):
    ctx, heads = mesh.shape["ctx"], mesh.shape["head"]
    X = 1 << ((ctx.bit_length() - 2) // 2)
    Z = ctx // 2 // X
    return jax.shard_map(
        functools.partial(shards, X, Z, heads),
        mesh=mesh,
        in_specs=(
            P("ctx", "head"),
            P("ctx", "head"),
            P("ctx", None),
            P("ctx", None),
            P("head", "ctx"),
            P(None, "head", "ctx"),
            P("head"),
            P("ctx", "head"),
            P("head", "ctx"),
        ),
        out_specs=(
            P("ctx", "head"),
            P("ctx", "head"),
            P("ctx", "head"),
            P("ctx", None),
            P("ctx", None),
            P("head", "ctx"),
            P(None, "head", "ctx"),
            P("head", "ctx"),
        ),
        check_vma=False,
    )
```

time: 89.9 us -> 76.7 us (0.85)
  local copies, waits for them, and re-layouts: 6.82 us -> 0 us
  Pallas kernels: 82 us -> 75.6 us
    pallas_call x1, Pallas kernels: 82 us -> 73.7 us  [shards(): pl.pallas_call(functools.partial(layer, (X, Z, Y, T, N, H, width)), out_s...]
    unnamed x22 -> x0, local copies, waits for them, and re-layouts: 6.82 us -> none
    pallas_call x0 -> x1, Pallas kernels: none -> 1.94 us  [shards(): pl.pallas_call(functools.partial(copy_out, len(results)), out_shape=tuple...]
where the time goes in v2:
time: 76.7 us; the launch traced here: 76.3 us
  Pallas kernels  75.6 us (99%)
    pallas_call x1, Pallas kernels, shards(): pl.pallas_call(functools.partial(layer, (X, Z, Y, T, N, H, width)), out_s...  73.7 us
    pallas_call x1, Pallas kernels, shards(): pl.pallas_call(functools.partial(copy_out, len(results)), out_shape=tuple...  1.94 us

profile of v2, /device:TPU:1, one launch (start us, length us, event | category | flops | bytes accessed | tf_op | source)
XLA Modules:
  0.0 76.3 jit_solution(15159969890436231364)
XLA Ops:
  0.6 73.7 %shard_map.152 = (bf16[128,512]{1,0:T(8,128)(2,1)}, bf16[128,512]{1,0:T(8,128)(2,1)}, bf16[128,512]{1,0:T(8,128)(2,1)}, f32[128,128]{1,0:T(8,128)}, f32[128,128]...) custom-call(bf16[128,512]{1,0:T(8,128)(2,1)} %v_ref.1, bf16[128,512]{1,0:T(8,128)(2,1)} %g_ref.1, ...), custom_call_target="tpu_custom_call" | custom-call | tf_op jit(solution)/shard_map/pallas_call | solution.py:748
  74.3 1.9 %shard_map.153 = (bf16[128,512]{1,0:T(8,128)(2,1)}, bf16[128,512]{1,0:T(8,128)(2,1)}, bf16[128,512]{1,0:T(8,128)(2,1)}, f32[128,128]{1,0:T(8,128)}, f32[128,128]...) custom-call(bf16[128,512]{1,0:T(8,128)(2,1)} %get-tuple-element.16.refs_0_, ...), custom_call_target="tpu_custom_call" | custom-call | tf_op jit(solution)/shard_map/pallas_call | solution.py:759

commit v3 on v2

--- a/solution.py
+++ b/solution.py
@@ -65,15 +65,16 @@
 
 def layer(
     sizes,
+    v_in, g_in, b_in, r_in, ld_in, ll_in, gain_in, ct_in, fc_in,
+    mixed_out, gv_out, gg_out, gw_out, gr_out, gd_out, gl_out, fs_out,
     v_ref, g_ref, b_ref, r_ref, ld_ref, ll_ref, gain_ref, ct_ref, fc_ref,
     mixed_ref, gv_ref, gg_ref, gw_ref, gr_ref, gd_ref, gl_ref, fs_ref,
-    fx, fd, fh, fl, silu_, slope, own_e, core_e, s1h, zr, zs, xr, xs, st,
+    fx, fd, fh, fl, silu_, slope, ss, s2, cols, go, own_e, core_e, s1h, zr, zs, xr, xs, st,
     wx, wp, md, ya, dl, dr, d0, dh, zb, d1, xbs, xb, gp, g1s, g1, gsc, gvl, gsm,
     t_own, t_core, t_pair, t_z, t_plane, t_x, f_own, f_x,
     v_own, v_core, v_pair, v_z, v_plane, v_x,
     n_own, n_y, part_r, rs_r, ag_r, own_r, part_w, rs_w, ag_w, own_w,
-    core_send, core_recv, z_send, z_recv, x_send, x_recv, y_send, y_recv,
-    down_send, down_recv, up_send, up_recv, pair_send, pair_recv,
+    send_sems, recv_sems, in_sems, out_sems,
 ):
     X, Z, Y, T, N, H, width = sizes
     C = H * width
@@ -95,32 +96,39 @@
     def device(x_, z_, k_, y_):
         return (x_ * (2 * Z) + z_ * 2 + k_, y_)
 
-    core_links = (core_send, core_recv, k, [(1 - k, device(x, z, 1 - k, y))])
-    z_links = (z_send, z_recv, z, [
-        (p, device(x, p, k, y)) for p in [(z + j) % Z for j in far_first(Z)]])
-    down_links = (down_send, down_recv) + z_links[2:]
-    up_links = (up_send, up_recv) + z_links[2:]
-    x_links = (x_send, x_recv, x, [
-        (p, device(p, z, k, y)) for p in [(x + j) % X for j in far_first(X)]])
-    y_links = (y_send, y_recv, y, [
-        (p, device(x, z, k, p)) for p in [(y + j) % Y for j in far_first(Y)]])
+    core_links = (k, [(1 - k, device(x, z, 1 - k, y))])
+    z_links = (z, [(p, device(x, p, k, y)) for p in [(z + j) % Z for j in far_first(Z)]])
+    x_links = (x, [(p, device(p, z, k, y)) for p in [(x + j) % X for j in far_first(X)]])
+    y_links = (y, [(p, device(x, z, k, p)) for p in [(y + j) % Y for j in far_first(Y)]])
     z_pair = z + 1 - 2 * (z % 2)
-    pair_links = (pair_send, pair_recv, 0, [(0, device(x, z_pair, k, y))])
+    pair_links = (0, [(0, device(x, z_pair, k, y))])
     all_z = [(z + j) % Z for j in far_first(Z) + [0]]
 
-    def plane_links(sends, recvs, plane):
-        return (sends, recvs, z, [(p, device(plane, p, k, y)) for p in all_z])
+    def plane_links(plane):
+        return (z, [(p, device(plane, p, k, y)) for p in all_z])
 
     next_plane = x + 1 - 2 * (x % 2)
     mirror_plane = X - 1 - x
 
     barrier = pltpu.get_barrier_semaphore()
-    peers = [dev for links in (core_links, z_links, x_links, y_links) for _, dev in links[3]]
-    peers += [device(next_plane, p, k, y) for p in all_z[:-1]]
-    if lx > 1:
-        peers += [device(mirror_plane, p, k, y) for p in all_z[:-1]]
+    peers = [dev for links in (core_links, z_links, x_links, y_links) for _, dev in links[1]]
     for peer in peers:
         pl.semaphore_signal(barrier, inc=1, device_id=peer, device_id_type=pl.DeviceIdType.MESH)
+
+    loads = {}
+    for n, (name, src, dst) in enumerate((
+        ("ld", ld_in, ld_ref), ("b", b_in, b_ref), ("v", v_in, v_ref), ("fc", fc_in, fc_ref),
+        ("r", r_in, r_ref), ("ll", ll_in, ll_ref), ("g", g_in, g_ref),
+        ("gain", gain_in, gain_ref), ("ct", ct_in, ct_ref),
+    )):
+        loads[name] = pltpu.make_async_copy(src, dst, in_sems.at[n])
+        loads[name].start()
+    stores = []
+
+    def store(src, dst):
+        item = pltpu.make_async_copy(src, dst, out_sems.at[len(stores)])
+        item.start()
+        stores.append(item)
 
     sent = []
 
@@ -130,26 +138,39 @@
         else:
             pl.when(cond)(action)
 
-    def exchange(links, slot, src_of, dst_of, send_if=lambda p: None, recv_if=lambda p: None):
-        send_sems, recv_sems, mine_, others = links
-
-        def item(n, src, dst, sender):
+    def exchange(links, src_of, dst_of, whole, send_if=lambda p: None, gone=None, got=None):
+        mine_, others = links
+        index = len(sent)
+        everyone = [(None, len(others))]
+
+        def item(src, dst, device_id):
             return pltpu.make_async_remote_copy(
-                src_ref=src, dst_ref=dst, send_sem=send_sems.at[slot, n],
-                recv_sem=recv_sems.at[slot, sender], device_id=others[n][1],
+                src_ref=src, dst_ref=dst, send_sem=send_sems.at[index],
+                recv_sem=recv_sems.at[index], device_id=device_id,
                 device_id_type=pl.DeviceIdType.MESH,
             )
 
-        for n, (p, _) in enumerate(others):
-            out = item(n, src_of(p), dst_of(mine_), mine_)
-            do(send_if(p), out.start)
-            sent.append((send_if(p), out.wait_send))
+        for p, device_id in others:
+            do(send_if(p), item(src_of(p), dst_of(mine_), device_id).start)
+
+        def wait_all(counts, kind):
+            for cond, count in counts:
+                if count:
+                    ref = whole(count)
+                    do(cond, getattr(item(ref, ref, others[0][1]), kind))
+
+        sent.append(lambda: wait_all(gone or everyone, "wait_send"))
 
         def wait():
-            for n, (p, _) in enumerate(others):
-                do(recv_if(p), item(n, dst_of(p), dst_of(p), p).wait_recv)
+            wait_all(got or everyone, "wait_recv")
 
         return wait
+
+    def slices(count):
+        return zr.at[0:count]
+
+    def half_of(condition):
+        return [(condition, Z // 2 - 1), (jnp.logical_not(condition), Z // 2)]
 
     def bit(index, place):
         return (index // 2**place) % 2 == 1
@@ -176,24 +197,24 @@
     natural = ((j_ % SR) // 2) * (4 * Z) + ((j_ % half) // SR) * 4 + (j_ // half) * 2 + j_ % 2
     order = jnp.where(natural == n_, 1.0, 0.0).astype(BF16)
 
-    write = b_ref[...]
-    read = r_ref[...]
-    write_p = mul(write, order, NT).astype(BF16)
-    write_t = mul(order, write, NT).astype(BF16)
-    read_p = mul(read, order, NT).astype(BF16)
-    read_t = mul(order, read, NT).astype(BF16)
 
     t_row = iota((T, T), 0)
     t_col = iota((T, T), 1)
     upto = jnp.where(t_row <= t_col, 1.0, 0.0)
+    loads["ld"].wait()
     cum = exact(ld_ref[...], upto)
     total = jnp.broadcast_to(cum[:, T - 1:T], (H, 128))
     t_own[...] = total
     fade = jnp.exp(cum[:, T - 1:T] - cum)
     fx[...] = spread_out(fade)
+    loads["b"].wait()
+    write = b_ref[...]
+    write_t = mul(order, write, NT).astype(BF16)
+    loads["v"].wait()
     faded = v_ref[...].astype(F32) * fx[...]
     fd[...] = faded
     own_e[...] = right_two(write_t, faded)
+    loads["fc"].wait()
     f_own[...] = fc_ref[...]
 
     @pl.when(k == 1)
@@ -202,14 +223,16 @@
 
     pl.semaphore_wait(barrier, len(peers))
 
-    wait_total = exchange(core_links, 0, lambda p: t_own, lambda p: t_core)
-    wait_end = exchange(core_links, 1, lambda p: own_e, lambda p: core_e)
-    wait_final = exchange(x_links, 0, lambda p: f_own, lambda p: f_x.at[p])
+    wait_total = exchange(core_links, lambda p: t_own, lambda p: t_core, lambda n: t_core)
+    wait_end = exchange(core_links, lambda p: own_e, lambda p: core_e, lambda n: core_e)
+    wait_final = exchange(
+        x_links, lambda p: f_own, lambda p: f_x.at[p], lambda n: f_x.at[0:n])
 
     wait_total()
     t_pair[...] = t_own[...] + t_core[...]
     t_z[z] = t_pair[...]
-    wait_pairs = exchange(z_links, 0, lambda p: t_pair, lambda p: t_z.at[p])
+    wait_pairs = exchange(
+        z_links, lambda p: t_pair, lambda p: t_z.at[p], lambda n: t_z.at[0:n])
 
     wait_end()
     upper_total = jnp.where(k == 1, t_own[...], t_core[...])
@@ -218,15 +241,22 @@
     from_core = (1.0 - kf) + kf * upper_decay
     mine = rows(k * half, half)
     s1h[...] = own_e[mine, :] * from_own + core_e[mine, :] * from_core
-    wait_slices = exchange(z_links, 1, lambda p: s1h.at[rows(p * SR, SR)], lambda p: zr.at[p])
+    wait_slices = exchange(
+        z_links, lambda p: s1h.at[rows(p * SR, SR)], lambda p: zr.at[p], slices)
     wait_state = [None] * slots
     wait_half = [None] * slots
     wait_state[0] = exchange(
-        pair_links, 0, lambda p: s1h, lambda p: st.at[0, mine],
-        lambda p: z % 2 == 0, lambda p: z % 2 == 1)
+        pair_links, lambda p: s1h, lambda p: st.at[0, mine], lambda n: s1h,
+        lambda p: z % 2 == 0, [(z % 2 == 0, 1)], [(z % 2 == 1, 1)])
     zr[z] = s1h[rows(z * SR, SR), :]
 
+    loads["r"].wait()
+    read = r_ref[...]
+    write_p = mul(write, order, NT).astype(BF16)
+    read_p = mul(read, order, NT).astype(BF16)
+    read_t = mul(order, read, NT).astype(BF16)
     scores = mul(read, write, NT)
+    loads["ll"].wait()
     cum_t = jnp.transpose(jnp.concatenate(
         [cum, ll_ref[0], ll_ref[1], jnp.zeros((128 - 3 * H, T), F32)], axis=0))
     later = t_row >= t_col
@@ -260,7 +290,8 @@
         tz.append([tz[i][2 * n] + tz[i][2 * n + 1] for n in range(Z >> (i + 1))])
     t_plane[...] = tz[lz][0]
     t_x[x] = tz[lz][0]
-    wait_plane_totals = exchange(x_links, 1, lambda p: t_plane, lambda p: t_x.at[p])
+    wait_plane_totals = exchange(
+        x_links, lambda p: t_plane, lambda p: t_x.at[p], lambda n: t_x.at[0:n])
     z_decay = [[wide(jnp.exp(tile)) for tile in level] for level in tz]
 
     local_pair(1)
@@ -279,21 +310,22 @@
 
     plane = z_nodes[lz].at[0]
     xr[x] = plane[...]
-    wait_planes = exchange(x_links, 2, lambda p: plane, lambda p: xr.at[p])
+    wait_planes = exchange(x_links, lambda p: plane, lambda p: xr.at[p], slices)
 
     def slice_of(slot):
         return lambda p: st.at[slot, rows(k * half + p * SR, SR)]
 
+    wait_plane_totals()
     wait_state[lz] = exchange(
-        plane_links(down_send, down_recv, next_plane), lz, lambda p: plane, slice_of(lz),
-        lambda p: x % 2 == 0, lambda p: x % 2 == 1)
+        plane_links(next_plane), lambda p: plane, slice_of(lz), slices,
+        lambda p: x % 2 == 0, [(x % 2 == 0, Z)], [(x % 2 == 1, Z)])
     for i in reversed(range(1, lz)):
         def below(p, i=i):
             return z_nodes[i].at[jnp.maximum(p // 2**i - 1, 0)]
 
         wait_state[i] = exchange(
-            down_links, i, below, slice_of(i), lambda p, i=i: bit(p, i),
-            lambda p, i=i: bit(z, i))
+            z_links, below, slice_of(i), slices, lambda p: bit(p, i),
+            half_of(bit(z, i)), [(bit(z, i), Z - 1)])
 
         @pl.when(bit(z, i))
         def _():
@@ -302,14 +334,13 @@
     def from_core_too(slot):
         wait_state[slot]()
         wait_half[slot] = exchange(
-            core_links, 2 + slot, lambda p: st.at[slot, mine],
-            lambda p: st.at[slot, rows(p * half, half)],
-            lambda p: needs(z, slot), lambda p: needs(z, slot))
+            core_links, lambda p: st.at[slot, mine], lambda p: st.at[slot, rows(p * half, half)],
+            lambda n: s1h, lambda p: needs(z, slot), [(needs(z, slot), 1)],
+            [(needs(z, slot), 1)])
 
     local_pair(2)
     from_core_too(0)
 
-    wait_plane_totals()
     tx = [[t_x[i] for i in range(X)]]
     for i in range(lx):
         tx.append([tx[i][2 * n] + tx[i][2 * n + 1] for n in range(X >> (i + 1))])
@@ -328,11 +359,11 @@
     if lx > 1:
         lower = x_nodes[1].at[0]
         wait_cross = exchange(
-            plane_links(down_send, down_recv, mirror_plane), lz + 1, lambda p: lower,
-            slice_of(lz + 1), lambda p: x == 1, lambda p: x == 2)
+            plane_links(mirror_plane), lambda p: lower, slice_of(lz + 1), slices,
+            lambda p: x == 1, [(x == 1, Z)], [(x == 2, Z)])
         wait_inside = exchange(
-            down_links, lz + 2, lambda p: lower, slice_of(lz + 1),
-            lambda p: x == 3, lambda p: x == 3)
+            z_links, lambda p: lower, slice_of(lz + 1), slices,
+            lambda p: x == 3, [(x == 3, Z - 1)], [(x == 3, Z - 1)])
 
         @pl.when(x == 3)
         def _():
@@ -391,10 +422,17 @@
         return tile + pltpu.roll(tile, width, 1)
 
     fs_ref[...] = jnp.where(tile_lane < width, narrow(2 * x), narrow(2 * x + 1))
-
+    store(fs_ref, fs_out)
+
+    loads["g"].wait()
     gate = g_ref[...].astype(F32)
     sigma = jax.nn.sigmoid(gate)
-    silu_[...] = gate * sigma
+    silu = gate * sigma
+    silu_[...] = silu
+    s2[...] = silu * silu
+    loads["gain"].wait()
+    loads["ct"].wait()
+    ss[...] = ct_ref[...].astype(F32) * gain_ref[...] * silu
     slope[...] = sigma * (1.0 + gate * (1.0 - sigma))
     faded_high, faded_low = split(fd[...])
     fh[...] = faded_high
@@ -407,33 +445,33 @@
     for slot in range(lz, slots):
         read_slot(slot)
 
-    silu = silu_[...]
     out = ya[...]
-    gated = out * silu
-    gain = gain_ref[...]
-    scaled = ct_ref[...].astype(F32) * gain
-    ones = jnp.ones((8, C), BF16)
-    squares = right_two(ones, gated * gated, NT)
-    inners = right_two(ones, scaled * gated, NT)
+
+    def folded(array):
+        tile = array[:, 0:128]
+        for n in range(1, C // 128):
+            tile = tile + array[:, n * 128:(n + 1) * 128]
+        return tile
+
+    ones = jnp.ones((8, 128), BF16)
+    squares = right_two(ones, folded(out * out * s2[...]), NT)
+    inners = right_two(ones, folded(out * ss[...]), NT)
     n_own[...] = jnp.where(iota((8, T), 0) == 0, squares, inners)
-    wait_norm = exchange(y_links, 0, lambda p: n_own, lambda p: n_y.at[p])
+    wait_norm = exchange(
+        y_links, lambda p: n_own, lambda p: n_y.at[p], lambda n: n_y.at[0:n])
+    n_y[y] = n_own[...]
     wait_norm()
-    n_y[y] = n_own[...]
     sums = n_y[0]
     for p in range(1, Y):
         sums = sums + n_y[p]
-    columns = jnp.transpose(jnp.concatenate([sums, jnp.zeros((120, T), F32)], axis=0))
-    inverse = lax.rsqrt(columns[:, 0:1] / channels + EPSILON)
-    inner = inverse * columns[:, 1:2]
-    normed = gated * inverse
-    mixed_ref[...] = (normed * gain).astype(BF16)
-    grad_gated = inverse * (scaled - normed * (inner / channels))
-    gg_ref[...] = (grad_gated * out * slope[...]).astype(BF16)
-    grad_out = grad_gated * silu
-    ya[...] = grad_out
+    inverse = lax.rsqrt(sums[0:1, :] / channels + EPSILON)
+    turn = inverse * inverse * (inverse * sums[1:2, :] / channels)
+    cols[...] = jnp.transpose(
+        jnp.concatenate([inverse, turn, jnp.zeros((126, T), F32)], axis=0))
+    go[...] = cols[:, 0:1] * ss[...] - cols[:, 1:2] * (out * s2[...])
 
     def state_grad(depth):
-        dl[depth] = right_two(read_t, ya[...] * wx[depth])
+        dl[depth] = right_two(read_t, go[...] * wx[depth])
 
     wait_core_grad = [None] * slots
     wait_grad = [None] * slots
@@ -445,8 +483,9 @@
             state_grad(1 + slot)
 
         wait_core_grad[slot] = exchange(
-            core_links, 2 + slots + slot, lambda p: dl.at[1 + slot, rows(p * half, half)],
-            lambda p: dr.at[slot], lambda p: needs(z, slot), lambda p: needs(z, slot))
+            core_links, lambda p: dl.at[1 + slot, rows(p * half, half)], lambda p: dr.at[slot],
+            lambda n: s1h, lambda p: needs(z, slot), [(needs(z, slot), 1)],
+            [(needs(z, slot), 1)])
 
     def finish_slot(slot):
         wait_core_grad[slot]()
@@ -460,16 +499,17 @@
 
         if slot == 0:
             wait_grad[0] = exchange(
-                pair_links, 1, lambda p: dh.at[0], lambda p: d1,
-                lambda p: z % 2 == 1, lambda p: z % 2 == 0)
+                pair_links, lambda p: dh.at[0], lambda p: d1, lambda n: s1h,
+                lambda p: z % 2 == 1, [(z % 2 == 1, 1)], [(z % 2 == 0, 1)])
         elif slot == lz:
             wait_grad[slot] = exchange(
-                plane_links(up_send, up_recv, next_plane), slot, piece, lambda p: zb.at[p, slot],
-                lambda p: x % 2 == 1, lambda p: x % 2 == 0)
+                plane_links(next_plane), piece, lambda p: zb.at[p, slot], slices,
+                lambda p: x % 2 == 1, [(x % 2 == 1, Z)], [(x % 2 == 0, Z)])
         else:
             wait_grad[slot] = exchange(
-                up_links, slot, piece, lambda p: zb.at[p, slot],
-                lambda p: needs(z, slot), lambda p: needs(p, slot))
+                z_links, piece, lambda p: zb.at[p, slot], slices,
+                lambda p: needs(z, slot), [(needs(z, slot), Z - 1)],
+                half_of(bit(z, slot)) if slot < lz else [(needs(z, slot), Z - 1)])
 
             @pl.when(needs(z, slot))
             def _():
@@ -486,8 +526,17 @@
 
     finish_slot(0)
     wait_lowest = exchange(
-        core_links, 2 + 2 * slots, lambda p: dl.at[0], lambda p: d0,
-        lambda p: k == 1, lambda p: k == 0)
+        core_links, lambda p: dl.at[0], lambda p: d0, lambda n: core_e,
+        lambda p: k == 1, [(k == 1, 1)], [(k == 0, 1)])
+
+    inverse, turn = cols[:, 0:1], cols[:, 1:2]
+    gated = ya[...] * silu_[...]
+    gain = gain_ref[...]
+    mixed_ref[...] = (gated * inverse * gain).astype(BF16)
+    store(mixed_ref, mixed_out)
+    grad_gated = inverse * (ct_ref[...].astype(F32) * gain) - turn * gated
+    gg_ref[...] = (grad_gated * ya[...] * slope[...]).astype(BF16)
+    store(gg_ref, gg_out)
 
     gsc[...] = jnp.zeros((T, T), F32)
     block_pick = jnp.where(
@@ -495,9 +544,9 @@
     late = iota((1, T), 1) >= BLOCK
 
     def backward_pair(pair):
-        cols = slice(pair * 128, (pair + 1) * 128)
-        vals = v_ref[:, cols]
-        grads = ya[:, cols]
+        lanes = slice(pair * 128, (pair + 1) * 128)
+        vals = v_ref[:, lanes]
+        grads = go[:, lanes]
         zero = jnp.zeros_like(grads)
         parts = [jnp.where(left, grads, zero), jnp.where(left, zero, grads)]
         kernels = []
@@ -513,7 +562,7 @@
             gl_ref[0, h:h + 1, :] = jnp.where(late, second, first)
             gl_ref[1, h:h + 1, :] = jnp.where(late, first, 0.0)
             gsm[h:h + 1, :] = first + second - jnp.sum(pulled, axis=0, keepdims=True)
-        gvl[:, cols] = both(
+        gvl[:, lanes] = both(
             jnp.concatenate(kernels, axis=0), jnp.concatenate(parts, axis=0), TN)
 
     backward_pair(0)
@@ -530,8 +579,8 @@
             xbs[...] = acc
 
         wait_plane_grads = exchange(
-            x_links, 3, lambda p: xbs, lambda p: xb.at[p],
-            lambda p: jnp.logical_and(x >= 2, p < 2), lambda p: jnp.logical_and(x < 2, p >= 2))
+            x_links, lambda p: xbs, lambda p: xb.at[p], slices,
+            lambda p: jnp.logical_and(x >= 2, p < 2), [(x >= 2, 2)], [(x < 2, 2)])
 
     backward_pair(2)
     backward_pair(3)
@@ -541,9 +590,9 @@
     pulled_all = jnp.zeros((H, T), F32)
 
     def level_back(depth, state):
-        weighted = ya[...] * wx[depth]
+        weighted = go[...] * wx[depth]
         part_r[...] = part_r[...] + both(weighted, state[...], NT)
-        gl_ref[2 + depth] = right_two(pick16, ya[...] * wp[depth], NT)
+        gl_ref[2 + depth] = right_two(pick16, go[...] * wp[depth], NT)
 
     for depth in range(cross):
         cond = (k == 1) if depth == 0 else needs(z, depth - 1)
@@ -556,9 +605,12 @@
         def _():
             gl_ref[2 + depth] = jnp.zeros((H, T), F32)
 
+    store(gl_ref, gl_out)
+
     chunk = T // Y
     wait_read_parts = exchange(
-        y_links, 1, lambda p: part_r.at[rows(p * chunk, chunk)], lambda p: rs_r.at[p])
+        y_links, lambda p: part_r.at[rows(p * chunk, chunk)], lambda p: rs_r.at[p],
+        lambda n: rs_r.at[0:n])
 
     wait_final()
     f_x[x] = f_own[...]
@@ -608,7 +660,7 @@
     for n in range(Z):
         g1s[n] = grads[n]
     wait_own_grad = exchange(
-        z_links, 2, lambda p: g1s.at[p], lambda p: g1.at[rows(k * half + p * SR, SR)])
+        z_links, lambda p: g1s.at[p], lambda p: g1.at[rows(k * half + p * SR, SR)], slices)
     g1[rows(k * half + z * SR, SR), :] = g1s[z]
 
     def own_chunk(part, received, own):
@@ -620,7 +672,8 @@
 
     wait_read_parts()
     own_chunk(part_r, rs_r, own_r)
-    wait_read = exchange(y_links, 2, lambda p: own_r, lambda p: ag_r.at[p])
+    wait_read = exchange(
+        y_links, lambda p: own_r, lambda p: ag_r.at[p], lambda n: ag_r.at[0:n])
     ag_r[y] = own_r[...]
 
     wait_own_grad()
@@ -630,35 +683,46 @@
     def _():
         g1[mine, :] = g1[mine, :] + d1[...]
 
-    last = 3 + 2 * slots
     wait_half_grad = exchange(
-        core_links, last, lambda p: g1.at[mine], lambda p: g1.at[rows(p * half, half)])
+        core_links, lambda p: g1.at[mine], lambda p: g1.at[rows(p * half, half)],
+        lambda n: s1h)
     wait_lowest()
     wait_half_grad()
 
     end_grad = g1[...] * from_own + d0[...]
+    pulled_all = gl_ref[2]
+    for depth in range(1, cross):
+        pulled_all = pulled_all + gl_ref[2 + depth]
+    passing = jnp.sum(pulled_all, axis=1, keepdims=True)
+    line = jnp.sum(own_e[...] * end_grad, axis=0, keepdims=True)
+    change = jnp.sum(jnp.where(pick, line, 0.0), axis=1, keepdims=True) - passing
+    v_own[...] = jnp.broadcast_to(change, (H, 128))
+    wait_change = exchange(core_links, lambda p: v_own, lambda p: v_core, lambda n: v_core)
     end_high, end_low = split(end_grad)
     part_w[...] = part_w[...] + (
         mul(fh[...], end_high, NT) + (mul(fl[...], end_high, NT) + mul(fh[...], end_low, NT)))
     wait_write_parts = exchange(
-        y_links, 3, lambda p: part_w.at[rows(p * chunk, chunk)], lambda p: rs_w.at[p])
-    spread = mul(write_p, end_high) + mul(write_p, end_low)
-    fade_pull = right_two(pick16, fd[...] * spread, NT)
-    pulled_all = gl_ref[2]
-    for depth in range(1, cross):
-        pulled_all = pulled_all + gl_ref[2 + depth]
-    passing = jnp.sum(pulled_all, axis=1, keepdims=True)
-    change = jnp.sum(fade_pull, axis=1, keepdims=True) - passing
-    v_own[...] = jnp.broadcast_to(change, (H, 128))
-    wait_change = exchange(core_links, last + 1, lambda p: v_own, lambda p: v_core)
-    gv_ref[...] = (gvl[...] + spread * fx[...]).astype(BF16)
+        y_links, lambda p: part_w.at[rows(p * chunk, chunk)], lambda p: rs_w.at[p],
+        lambda n: rs_w.at[0:n])
     wait_change()
     v_pair[...] = v_own[...] + v_core[...]
-    wait_changes = exchange(z_links, 3, lambda p: v_pair, lambda p: v_z.at[p])
+    wait_changes = exchange(
+        z_links, lambda p: v_pair, lambda p: v_z.at[p], lambda n: v_z.at[0:n])
+    spread = mul(write_p, end_high) + mul(write_p, end_low)
+    gv_ref[...] = (gvl[...] + spread * fx[...]).astype(BF16)
+    store(gv_ref, gv_out)
+    fade_pull = right_two(pick16, fd[...] * spread, NT)
+    within = exact(pulled_all + gsm[...], jnp.where(t_row >= t_col, 1.0, 0.0))
+    within = within + exact(fade_pull, jnp.where(t_row < t_col, 1.0, 0.0)) - passing
+    wait_read()
+    for p in range(Y):
+        gr_ref[p * chunk:(p + 1) * chunk, :] = ag_r[p]
+    store(gr_ref, gr_out)
 
     wait_write_parts()
     own_chunk(part_w, rs_w, own_w)
-    wait_write = exchange(y_links, 4, lambda p: own_w, lambda p: ag_w.at[p])
+    wait_write = exchange(
+        y_links, lambda p: own_w, lambda p: ag_w.at[p], lambda n: ag_w.at[0:n])
     ag_w[y] = own_w[...]
 
     passed = jnp.where(k == 1, v_core[...], 0.0)
@@ -670,24 +734,23 @@
         in_plane = in_plane + tile
         passed = passed + jnp.where(z > p, tile, 0.0)
     v_plane[...] = in_plane
-    wait_plane_changes = exchange(x_links, 4, lambda p: v_plane, lambda p: v_x.at[p])
-    within = exact(pulled_all + gsm[...], jnp.where(t_row >= t_col, 1.0, 0.0))
-    within = within + exact(fade_pull, jnp.where(t_row < t_col, 1.0, 0.0)) - passing
+    wait_plane_changes = exchange(
+        x_links, lambda p: v_plane, lambda p: v_x.at[p], lambda n: v_x.at[0:n])
     wait_plane_changes()
     v_x[x] = in_plane
     for p in range(X):
         passed = passed + jnp.where(x > p, v_x[p], 0.0)
     gd_ref[...] = within + passed[:, 0:1]
-
-    wait_read()
-    for p in range(Y):
-        gr_ref[p * chunk:(p + 1) * chunk, :] = ag_r[p]
+    store(gd_ref, gd_out)
     wait_write()
     for p in range(Y):
         gw_ref[p * chunk:(p + 1) * chunk, :] = ag_w[p]
-
-    for cond, wait_send in sent:
-        do(cond, wait_send)
+    store(gw_ref, gw_out)
+    for item in stores:
+        item.wait()
+
+    for wait_sent in sent:
+        wait_sent()
 
 
 def copy_out(count, *refs):
@@ -717,9 +780,15 @@
         return pltpu.VMEM(shape, dtype)
 
     sem = pltpu.SemaphoreType.DMA
+    outs = (
+        ((T, C), BF16), ((T, C), BF16), ((T, C), BF16), ((T, N), F32), ((T, N), F32),
+        ((H, T), F32), (logit.shape, F32), (final_cot.shape, F32),
+    )
+    args = (values, gate, write, read, decay, logit, gain.reshape(1, C), cot, final_cot)
     scratch = dict(
         fx=mem(T, C), fd=mem(T, C), fh=mem(T, C, dtype=BF16), fl=mem(T, C, dtype=BF16),
-        silu_=mem(T, C), slope=mem(T, C), own_e=mem(N, C), core_e=mem(N, C),
+        silu_=mem(T, C), slope=mem(T, C), ss=mem(T, C), s2=mem(T, C), cols=mem(T, 128),
+        go=mem(T, C), own_e=mem(N, C), core_e=mem(N, C),
         s1h=mem(half, C), zr=mem(Z, SR, C), zs=mem(Z - 1, SR, C),
         xr=mem(X, SR, C), xs=mem(X - 1, SR, C), st=mem(slots, N, C),
         wx=mem(cross, T, C), wp=mem(cross, T, C), md=mem(H, T, T), ya=mem(T, C),
@@ -733,29 +802,23 @@
         n_own=mem(8, T), n_y=mem(Y, 8, T),
         part_r=mem(T, N), rs_r=mem(Y, chunk, N), ag_r=mem(Y, chunk, N), own_r=mem(chunk, N),
         part_w=mem(T, N), rs_w=mem(Y, chunk, N), ag_w=mem(Y, chunk, N), own_w=mem(chunk, N),
-        core_send=sem((5 + 2 * slots, 1)), core_recv=sem((5 + 2 * slots, 2)),
-        z_send=sem((4, Z)), z_recv=sem((4, Z)), x_send=sem((5, X)), x_recv=sem((5, X)),
-        y_send=sem((5, Y)), y_recv=sem((5, Y)),
-        down_send=sem((slots + 1, Z)), down_recv=sem((slots + 1, Z)),
-        up_send=sem((slots, Z)), up_recv=sem((slots, Z)),
-        pair_send=sem((2, 1)), pair_recv=sem((2, 1)),
+        send_sems=sem((24 + 4 * slots,)), recv_sems=sem((24 + 4 * slots,)),
+        in_sems=sem((9,)), out_sems=sem((8,)),
     )
     vmem = pl.BlockSpec(memory_space=pltpu.VMEM)
-    outs = (
-        ((T, C), BF16), ((T, C), BF16), ((T, C), BF16), ((T, N), F32), ((T, N), F32),
-        ((H, T), F32), (logit.shape, F32), (final_cot.shape, F32),
-    )
+    anywhere = pl.BlockSpec(memory_space=pl.ANY)
     results = pl.pallas_call(
         functools.partial(layer, (X, Z, Y, T, N, H, width)),
         out_shape=tuple(jax.ShapeDtypeStruct(shape, dtype) for shape, dtype in outs),
-        in_specs=[vmem] * 9,
-        out_specs=(vmem,) * 8,
-        scratch_shapes=list(scratch.values()),
+        in_specs=[anywhere] * len(args),
+        out_specs=(anywhere,) * len(outs),
+        scratch_shapes=(
+            [mem(*a.shape, dtype=a.dtype) for a in args]
+            + [mem(*shape, dtype=dtype) for shape, dtype in outs] + list(scratch.values())),
         compiler_params=pltpu.CompilerParams(
             collective_id=0, has_side_effects=True, vmem_limit_bytes=56 * 2**20
         ),
-    )(values, gate, write, read, decay, logit, gain.reshape(1, C), cot, final_cot)
-    anywhere = pl.BlockSpec(memory_space=pl.ANY)
+    )(*args)
     return pl.pallas_call(
         functools.partial(copy_out, len(results)),
         out_shape=tuple(jax.ShapeDtypeStruct(shape, dtype) for shape, dtype in outs),

time: 76.7 us -> 73.4 us (0.957)
  Pallas kernels: 75.6 us -> 72.2 us
    pallas_call x1, Pallas kernels: 73.7 us -> 70.2 us  [shards(): pl.pallas_call(functools.partial(layer, (X, Z, Y, T, N, H, width)), out_s...]
where the time goes in v3:
time: 73.4 us; the launch traced here: 72.8 us
  Pallas kernels  72.2 us (98%)
    pallas_call x1, Pallas kernels, shards(): pl.pallas_call(functools.partial(layer, (X, Z, Y, T, N, H, width)), out_s...  70.2 us
    pallas_call x1, Pallas kernels, shards(): pl.pallas_call(functools.partial(copy_out, len(results)), out_shape=tuple...  1.94 us

profile of v3, /device:TPU:1, one launch (start us, length us, event | category | flops | bytes accessed | tf_op | source)
XLA Modules:
  0.0 72.8 jit_solution(7024542788184057997)
XLA Ops:
  0.6 70.2 %shard_map.152 = (bf16[128,512]{1,0:T(8,128)(2,1)}, bf16[128,512]{1,0:T(8,128)(2,1)}, bf16[128,512]{1,0:T(8,128)(2,1)}, f32[128,128]{1,0:T(8,128)}, f32[128,128]...) custom-call(bf16[128,512]{1,0:T(8,128)(2,1)} %v_in.1, bf16[128,512]{1,0:T(8,128)(2,1)} %g_in.1, ...), custom_call_target="tpu_custom_call" | custom-call | tf_op jit(solution)/shard_map/pallas_call | solution.py:810
  70.9 1.9 %shard_map.153 = (bf16[128,512]{1,0:T(8,128)(2,1)}, bf16[128,512]{1,0:T(8,128)(2,1)}, bf16[128,512]{1,0:T(8,128)(2,1)}, f32[128,128]{1,0:T(8,128)}, f32[128,128]...) custom-call(bf16[128,512]{1,0:T(8,128)(2,1)} %get-tuple-element.16.refs_0_, ...), custom_call_target="tpu_custom_call" | custom-call | tf_op jit(solution)/shard_map/pallas_call | solution.py:822

commit v4 on v3

--- a/solution.py
+++ b/solution.py
@@ -69,11 +69,11 @@
     mixed_out, gv_out, gg_out, gw_out, gr_out, gd_out, gl_out, fs_out,
     v_ref, g_ref, b_ref, r_ref, ld_ref, ll_ref, gain_ref, ct_ref, fc_ref,
     mixed_ref, gv_ref, gg_ref, gw_ref, gr_ref, gd_ref, gl_ref, fs_ref,
-    fx, fd, fh, fl, silu_, slope, ss, s2, cols, go, own_e, core_e, s1h, zr, zs, xr, xs, st,
+    fx, fd, fh, fl, silu_, slope, ss, s2, cols, go, rt, gh, gl2, own_e, core_e, s1h, s1t, zr, zs, plane_t, xr, xs, st,
     wx, wp, md, ya, dl, dr, d0, dh, zb, d1, xbs, xb, gp, g1s, g1, gsc, gvl, gsm,
-    t_own, t_core, t_pair, t_z, t_plane, t_x, f_own, f_x,
+    t_own, t_core, f_own, f_x,
     v_own, v_core, v_pair, v_z, v_plane, v_x,
-    n_own, n_y, part_r, rs_r, ag_r, own_r, part_w, rs_w, ag_w, own_w,
+    n_own, n_y, part_r, rs_r, own_r, part_w, rs_w, own_w,
     send_sems, recv_sems, in_sems, out_sems,
 ):
     X, Z, Y, T, N, H, width = sizes
@@ -167,7 +167,7 @@
         return wait
 
     def slices(count):
-        return zr.at[0:count]
+        return g1s.at[0:count]
 
     def half_of(condition):
         return [(condition, Z // 2 - 1), (jnp.logical_not(condition), Z // 2)]
@@ -224,37 +224,44 @@
     pl.semaphore_wait(barrier, len(peers))
 
     wait_total = exchange(core_links, lambda p: t_own, lambda p: t_core, lambda n: t_core)
-    wait_end = exchange(core_links, lambda p: own_e, lambda p: core_e, lambda n: core_e)
-    wait_final = exchange(
-        x_links, lambda p: f_own, lambda p: f_x.at[p], lambda n: f_x.at[0:n])
-
+    wait_end = exchange(
+        core_links, lambda p: own_e.at[rows(p * half, half)],
+        lambda p: core_e.at[rows((1 - p) * half, half)], lambda n: s1h)
     wait_total()
-    t_pair[...] = t_own[...] + t_core[...]
-    t_z[z] = t_pair[...]
-    wait_pairs = exchange(
-        z_links, lambda p: t_pair, lambda p: t_z.at[p], lambda n: t_z.at[0:n])
-
-    wait_end()
     upper_total = jnp.where(k == 1, t_own[...], t_core[...])
     upper_decay = wide(jnp.exp(upper_total))
     from_own = kf + (1.0 - kf) * upper_decay
     from_core = (1.0 - kf) + kf * upper_decay
     mine = rows(k * half, half)
-    s1h[...] = own_e[mine, :] * from_own + core_e[mine, :] * from_core
+    chip_total = t_own[...] + t_core[...]
+    for n in range(Z):
+        s1t[n, :, C:] = chip_total
+
+    wait_end()
+    merged = own_e[mine, :] * from_own + core_e[mine, :] * from_core
+    for n in range(Z):
+        s1t[n, :, :C] = merged[n * SR:(n + 1) * SR, :]
     wait_slices = exchange(
-        z_links, lambda p: s1h.at[rows(p * SR, SR)], lambda p: zr.at[p], slices)
+        z_links, lambda p: s1t.at[p], lambda p: zr.at[p], lambda n: zr.at[0:n])
+    s1h[...] = merged
     wait_state = [None] * slots
     wait_half = [None] * slots
+    wait_final = exchange(
+        x_links, lambda p: f_own, lambda p: f_x.at[p], lambda n: f_x.at[0:n])
     wait_state[0] = exchange(
         pair_links, lambda p: s1h, lambda p: st.at[0, mine], lambda n: s1h,
         lambda p: z % 2 == 0, [(z % 2 == 0, 1)], [(z % 2 == 1, 1)])
-    zr[z] = s1h[rows(z * SR, SR), :]
+    zr[z] = s1t[z]
+    wait_other_end = exchange(
+        core_links, lambda p: own_e.at[0:half], lambda p: core_e.at[0:half], lambda n: s1h,
+        lambda p: k == 0, [(k == 0, 1)], [(k == 1, 1)])
 
     loads["r"].wait()
     read = r_ref[...]
     write_p = mul(write, order, NT).astype(BF16)
     read_p = mul(read, order, NT).astype(BF16)
     read_t = mul(order, read, NT).astype(BF16)
+    rt[...] = read_t
     scores = mul(read, write, NT)
     loads["ll"].wait()
     cum_t = jnp.transpose(jnp.concatenate(
@@ -284,19 +291,21 @@
 
     local_pair(0)
 
-    wait_pairs()
-    tz = [[t_z[i] for i in range(Z)]]
-    for i in range(lz):
-        tz.append([tz[i][2 * n] + tz[i][2 * n + 1] for n in range(Z >> (i + 1))])
-    t_plane[...] = tz[lz][0]
-    t_x[x] = tz[lz][0]
-    wait_plane_totals = exchange(
-        x_links, lambda p: t_plane, lambda p: t_x.at[p], lambda n: t_x.at[0:n])
-    z_decay = [[wide(jnp.exp(tile)) for tile in level] for level in tz]
-
     local_pair(1)
 
     wait_slices()
+
+    def tree_totals(tiles):
+        levels = [tiles]
+        while len(levels[-1]) > 1:
+            last = levels[-1]
+            levels.append([last[n] + last[n + 1] for n in range(0, len(last), 2)])
+        decays = [
+            [wide(jnp.exp(tile)) if n % 2 else None for n, tile in enumerate(level)]
+            for level in levels[:-1]]
+        return levels, decays
+
+    tz, z_decay = tree_totals([zr[n, :, C:] for n in range(Z)])
     z_nodes = [zr]
     base = 0
     for i in range(lz):
@@ -304,18 +313,21 @@
         count = Z >> (i + 1)
         there = zs.at[base:base + count]
         for n in range(count):
-            there[n] = here[2 * n] * z_decay[i][2 * n + 1] + here[2 * n + 1]
+            there[n] = here[2 * n, :, :C] * z_decay[i][2 * n + 1] + here[2 * n + 1, :, :C]
         z_nodes.append(there)
         base += count
 
     plane = z_nodes[lz].at[0]
-    xr[x] = plane[...]
-    wait_planes = exchange(x_links, lambda p: plane, lambda p: xr.at[p], slices)
+    plane_t[:, :C] = plane[...]
+    plane_t[:, C:] = tz[lz][0]
+    wait_planes = exchange(
+        x_links, lambda p: plane_t, lambda p: xr.at[p], lambda n: xr.at[0:n])
+    xr[x] = plane_t[...]
 
     def slice_of(slot):
         return lambda p: st.at[slot, rows(k * half + p * SR, SR)]
 
-    wait_plane_totals()
+    wait_final()
     wait_state[lz] = exchange(
         plane_links(next_plane), lambda p: plane, slice_of(lz), slices,
         lambda p: x % 2 == 0, [(x % 2 == 0, Z)], [(x % 2 == 1, Z)])
@@ -341,11 +353,8 @@
     local_pair(2)
     from_core_too(0)
 
-    tx = [[t_x[i] for i in range(X)]]
-    for i in range(lx):
-        tx.append([tx[i][2 * n] + tx[i][2 * n + 1] for n in range(X >> (i + 1))])
-    x_decay = [[wide(jnp.exp(tile)) for tile in level] for level in tx]
     wait_planes()
+    tx, x_decay = tree_totals([xr[n, :, C:] for n in range(X)])
     x_nodes = [xr]
     base = 0
     for i in range(lx):
@@ -353,7 +362,7 @@
         count = X >> (i + 1)
         there = xs.at[base:base + count]
         for n in range(count):
-            there[n] = here[2 * n] * x_decay[i][2 * n + 1] + here[2 * n + 1]
+            there[n] = here[2 * n, :, :C] * x_decay[i][2 * n + 1] + here[2 * n + 1, :, :C]
         x_nodes.append(there)
         base += count
     if lx > 1:
@@ -402,6 +411,8 @@
         @pl.when(needs(z, slot))
         def _():
             read_level(1 + slot, st.at[slot])
+
+    wait_other_end()
 
     @pl.when(k == 1)
     def _():
@@ -473,6 +484,10 @@
     def state_grad(depth):
         dl[depth] = right_two(read_t, go[...] * wx[depth])
 
+    def half_grad(depth, part):
+        read_half = rt[part, :]
+        dl[depth, part, :] = mul(read_half, gh[...]) + mul(read_half, gl2[...])
+
     wait_core_grad = [None] * slots
     wait_grad = [None] * slots
     other = rows((1 - k) * half, half)
@@ -480,12 +495,19 @@
     def start_slot(slot):
         @pl.when(needs(z, slot))
         def _():
-            state_grad(1 + slot)
+            high, low = split(go[...] * wx[1 + slot])
+            gh[...] = high
+            gl2[...] = low
+            half_grad(1 + slot, other)
 
         wait_core_grad[slot] = exchange(
             core_links, lambda p: dl.at[1 + slot, rows(p * half, half)], lambda p: dr.at[slot],
             lambda n: s1h, lambda p: needs(z, slot), [(needs(z, slot), 1)],
             [(needs(z, slot), 1)])
+
+        @pl.when(needs(z, slot))
+        def _():
+            half_grad(1 + slot, mine)
 
     def finish_slot(slot):
         wait_core_grad[slot]()
@@ -612,7 +634,6 @@
         y_links, lambda p: part_r.at[rows(p * chunk, chunk)], lambda p: rs_r.at[p],
         lambda n: rs_r.at[0:n])
 
-    wait_final()
     f_x[x] = f_own[...]
     grad = jnp.zeros((SR, C), F32)
     for n in range(X):
@@ -673,8 +694,9 @@
     wait_read_parts()
     own_chunk(part_r, rs_r, own_r)
     wait_read = exchange(
-        y_links, lambda p: own_r, lambda p: ag_r.at[p], lambda n: ag_r.at[0:n])
-    ag_r[y] = own_r[...]
+        y_links, lambda p: own_r, lambda p: gr_ref.at[rows(p * chunk, chunk)],
+        lambda n: rs_r.at[0:n])
+    gr_ref[rows(y * chunk, chunk), :] = own_r[...]
 
     wait_own_grad()
     wait_grad[0]()
@@ -690,6 +712,12 @@
     wait_half_grad()
 
     end_grad = g1[...] * from_own + d0[...]
+    end_high, end_low = split(end_grad)
+    part_w[...] = part_w[...] + (
+        mul(fh[...], end_high, NT) + (mul(fl[...], end_high, NT) + mul(fh[...], end_low, NT)))
+    wait_write_parts = exchange(
+        y_links, lambda p: part_w.at[rows(p * chunk, chunk)], lambda p: rs_w.at[p],
+        lambda n: rs_w.at[0:n])
     pulled_all = gl_ref[2]
     for depth in range(1, cross):
         pulled_all = pulled_all + gl_ref[2 + depth]
@@ -698,12 +726,6 @@
     change = jnp.sum(jnp.where(pick, line, 0.0), axis=1, keepdims=True) - passing
     v_own[...] = jnp.broadcast_to(change, (H, 128))
     wait_change = exchange(core_links, lambda p: v_own, lambda p: v_core, lambda n: v_core)
-    end_high, end_low = split(end_grad)
-    part_w[...] = part_w[...] + (
-        mul(fh[...], end_high, NT) + (mul(fl[...], end_high, NT) + mul(fh[...], end_low, NT)))
-    wait_write_parts = exchange(
-        y_links, lambda p: part_w.at[rows(p * chunk, chunk)], lambda p: rs_w.at[p],
-        lambda n: rs_w.at[0:n])
     wait_change()
     v_pair[...] = v_own[...] + v_core[...]
     wait_changes = exchange(
@@ -715,15 +737,14 @@
     within = exact(pulled_all + gsm[...], jnp.where(t_row >= t_col, 1.0, 0.0))
     within = within + exact(fade_pull, jnp.where(t_row < t_col, 1.0, 0.0)) - passing
     wait_read()
-    for p in range(Y):
-        gr_ref[p * chunk:(p + 1) * chunk, :] = ag_r[p]
     store(gr_ref, gr_out)
 
     wait_write_parts()
     own_chunk(part_w, rs_w, own_w)
     wait_write = exchange(
-        y_links, lambda p: own_w, lambda p: ag_w.at[p], lambda n: ag_w.at[0:n])
-    ag_w[y] = own_w[...]
+        y_links, lambda p: own_w, lambda p: gw_ref.at[rows(p * chunk, chunk)],
+        lambda n: rs_w.at[0:n])
+    gw_ref[rows(y * chunk, chunk), :] = own_w[...]
 
     passed = jnp.where(k == 1, v_core[...], 0.0)
     wait_changes()
@@ -743,8 +764,6 @@
     gd_ref[...] = within + passed[:, 0:1]
     store(gd_ref, gd_out)
     wait_write()
-    for p in range(Y):
-        gw_ref[p * chunk:(p + 1) * chunk, :] = ag_w[p]
     store(gw_ref, gw_out)
     for item in stores:
         item.wait()
@@ -754,13 +773,20 @@
 
 
 def copy_out(count, *refs):
-    sems = refs[2 * count]
-    copies = [
-        pltpu.make_async_copy(refs[n], refs[count + n], sems.at[n]) for n in range(count)
+    sources, targets, held = (refs[n * count:(n + 1) * count] for n in range(3))
+    sems = refs[3 * count]
+    loads = [
+        pltpu.make_async_copy(sources[n], held[n], sems.at[0, n]) for n in range(count)
     ]
-    for item in copies:
+    stores = [
+        pltpu.make_async_copy(held[n], targets[n], sems.at[1, n]) for n in range(count)
+    ]
+    for item in loads:
         item.start()
-    for item in copies:
+    for load, item in zip(loads, stores):
+        load.wait()
+        item.start()
+    for item in stores:
         item.wait()
 
 
@@ -788,24 +814,23 @@
     scratch = dict(
         fx=mem(T, C), fd=mem(T, C), fh=mem(T, C, dtype=BF16), fl=mem(T, C, dtype=BF16),
         silu_=mem(T, C), slope=mem(T, C), ss=mem(T, C), s2=mem(T, C), cols=mem(T, 128),
-        go=mem(T, C), own_e=mem(N, C), core_e=mem(N, C),
-        s1h=mem(half, C), zr=mem(Z, SR, C), zs=mem(Z - 1, SR, C),
-        xr=mem(X, SR, C), xs=mem(X - 1, SR, C), st=mem(slots, N, C),
+        go=mem(T, C), rt=mem(N, T, dtype=BF16), gh=mem(T, C, dtype=BF16),
+        gl2=mem(T, C, dtype=BF16), own_e=mem(N, C), core_e=mem(N, C),
+        s1h=mem(half, C), s1t=mem(Z, SR, C + 128), zr=mem(Z, SR, C + 128), zs=mem(Z - 1, SR, C),
+        plane_t=mem(SR, C + 128), xr=mem(X, SR, C + 128), xs=mem(X - 1, SR, C), st=mem(slots, N, C),
         wx=mem(cross, T, C), wp=mem(cross, T, C), md=mem(H, T, T), ya=mem(T, C),
         dl=mem(cross, N, C), dr=mem(slots, half, C), d0=mem(N, C), dh=mem(slots, half, C),
         zb=mem(Z, slots, SR, C), d1=mem(half, C), xbs=mem(SR, C), xb=mem(X, SR, C),
         gp=mem(SR, C), g1s=mem(Z, SR, C), g1=mem(N, C), gsc=mem(T, T), gvl=mem(T, C), gsm=mem(H, T),
-        t_own=mem(H, 128), t_core=mem(H, 128), t_pair=mem(H, 128), t_z=mem(Z, H, 128),
-        t_plane=mem(H, 128), t_x=mem(X, H, 128), f_own=mem(H, 128), f_x=mem(X, H, 128),
+        t_own=mem(H, 128), t_core=mem(H, 128), f_own=mem(H, 128), f_x=mem(X, H, 128),
         v_own=mem(H, 128), v_core=mem(H, 128), v_pair=mem(H, 128), v_z=mem(Z, H, 128),
         v_plane=mem(H, 128), v_x=mem(X, H, 128),
         n_own=mem(8, T), n_y=mem(Y, 8, T),
-        part_r=mem(T, N), rs_r=mem(Y, chunk, N), ag_r=mem(Y, chunk, N), own_r=mem(chunk, N),
-        part_w=mem(T, N), rs_w=mem(Y, chunk, N), ag_w=mem(Y, chunk, N), own_w=mem(chunk, N),
+        part_r=mem(T, N), rs_r=mem(Y, chunk, N), own_r=mem(chunk, N),
+        part_w=mem(T, N), rs_w=mem(Y, chunk, N), own_w=mem(chunk, N),
         send_sems=sem((24 + 4 * slots,)), recv_sems=sem((24 + 4 * slots,)),
         in_sems=sem((9,)), out_sems=sem((8,)),
     )
-    vmem = pl.BlockSpec(memory_space=pltpu.VMEM)
     anywhere = pl.BlockSpec(memory_space=pl.ANY)
     results = pl.pallas_call(
         functools.partial(layer, (X, Z, Y, T, N, H, width)),
@@ -822,9 +847,11 @@
     return pl.pallas_call(
         functools.partial(copy_out, len(results)),
         out_shape=tuple(jax.ShapeDtypeStruct(shape, dtype) for shape, dtype in outs),
-        in_specs=[vmem] * len(results),
+        in_specs=[anywhere] * len(results),
         out_specs=(anywhere,) * len(results),
-        scratch_shapes=[sem((len(results),))],
+        scratch_shapes=(
+            [mem(*shape, dtype=dtype) for shape, dtype in outs] + [sem((2, len(results)))]),
+        compiler_params=pltpu.CompilerParams(vmem_limit_bytes=56 * 2**20),
     )(*results)
 
 

time: 73.4 us -> 72.6 us (0.989)
  no operation moved by 1% of the time
where the time goes in v4:
time: 72.6 us; the launch traced here: 72.2 us
  Pallas kernels  71.6 us (99%)
    pallas_call x1, Pallas kernels, shards(): pl.pallas_call(functools.partial(layer, (X, Z, Y, T, N, H, width)), out_s...  69.7 us
    pallas_call x1, Pallas kernels, shards(): pl.pallas_call(functools.partial(copy_out, len(results)), out_shape=tuple...  1.88 us

profile of v4, /device:TPU:1, one launch (start us, length us, event | category | flops | bytes accessed | tf_op | source)
XLA Modules:
  0.0 72.2 jit_solution(16158938794315817975)
XLA Ops:
  0.6 69.7 %shard_map.152 = (bf16[128,512]{1,0:T(8,128)(2,1)}, bf16[128,512]{1,0:T(8,128)(2,1)}, bf16[128,512]{1,0:T(8,128)(2,1)}, f32[128,128]{1,0:T(8,128)}, f32[128,128]...) custom-call(bf16[128,512]{1,0:T(8,128)(2,1)} %v_in.1, bf16[128,512]{1,0:T(8,128)(2,1)} %g_in.1, ...), custom_call_target="tpu_custom_call" | custom-call | tf_op jit(solution)/shard_map/pallas_call | solution.py:835
  70.3 1.9 %shard_map.153 = (bf16[128,512]{1,0:T(8,128)(2,1)}, bf16[128,512]{1,0:T(8,128)(2,1)}, bf16[128,512]{1,0:T(8,128)(2,1)}, f32[128,128]{1,0:T(8,128)}, f32[128,128]...) custom-call(bf16[128,512]{1,0:T(8,128)(2,1)} %get-tuple-element.16.refs_0_, ...), custom_call_target="tpu_custom_call" | custom-call | tf_op jit(solution)/shard_map/pallas_call | solution.py:847

commit v5 on v4

--- a/solution.py
+++ b/solution.py
@@ -111,7 +111,11 @@
     mirror_plane = X - 1 - x
 
     barrier = pltpu.get_barrier_semaphore()
-    peers = [dev for links in (core_links, z_links, x_links, y_links) for _, dev in links[1]]
+    lines = [(z_links, Z), (y_links, Y), (x_links, X), (core_links, 2)]
+    peers = [
+        (-min(j, size - j), dev)
+        for links, size in lines for j, (_, dev) in zip(far_first(size), links[1])]
+    peers = [dev for _, dev in sorted(peers, key=lambda pair: pair[0])]
     for peer in peers:
         pl.semaphore_signal(barrier, inc=1, device_id=peer, device_id_type=pl.DeviceIdType.MESH)
 
@@ -757,6 +761,12 @@
     v_plane[...] = in_plane
     wait_plane_changes = exchange(
         x_links, lambda p: v_plane, lambda p: v_x.at[p], lambda n: v_x.at[0:n])
+    assert len(sent) == send_sems.shape[0]
+    settled, stored = len(sent) - 2, len(stores)
+    for wait_sent in sent[:settled]:
+        wait_sent()
+    for item in stores:
+        item.wait()
     wait_plane_changes()
     v_x[x] = in_plane
     for p in range(X):
@@ -765,11 +775,10 @@
     store(gd_ref, gd_out)
     wait_write()
     store(gw_ref, gw_out)
-    for item in stores:
+    for wait_sent in sent[settled:]:
+        wait_sent()
+    for item in stores[stored:]:
         item.wait()
-
-    for wait_sent in sent:
-        wait_sent()
 
 
 def copy_out(count, *refs):
@@ -801,6 +810,7 @@
     slots = lz + lx
     cross = 1 + slots
     chunk = T // Y
+    exchanges = 18 + 3 * slots + lz + (3 if lx > 1 else 0)
 
     def mem(*shape, dtype=F32):
         return pltpu.VMEM(shape, dtype)
@@ -828,7 +838,7 @@
         n_own=mem(8, T), n_y=mem(Y, 8, T),
         part_r=mem(T, N), rs_r=mem(Y, chunk, N), own_r=mem(chunk, N),
         part_w=mem(T, N), rs_w=mem(Y, chunk, N), own_w=mem(chunk, N),
-        send_sems=sem((24 + 4 * slots,)), recv_sems=sem((24 + 4 * slots,)),
+        send_sems=sem((exchanges,)), recv_sems=sem((exchanges,)),
         in_sems=sem((9,)), out_sems=sem((8,)),
     )
     anywhere = pl.BlockSpec(memory_space=pl.ANY)

time: 72.6 us -> 72.6 us (level)
  no operation moved by 1% of the time
where the time goes in v5:
time: 72.6 us; the launch traced here: 72 us
  Pallas kernels  71.4 us (98%)
    pallas_call x1, Pallas kernels, shards(): pl.pallas_call(functools.partial(layer, (X, Z, Y, T, N, H, width)), out_s...  69.5 us
    pallas_call x1, Pallas kernels, shards(): pl.pallas_call(functools.partial(copy_out, len(results)), out_shape=tuple...  1.88 us

profile of v5, /device:TPU:1, one launch (start us, length us, event | category | flops | bytes accessed | tf_op | source)
XLA Modules:
  0.0 72.0 jit_solution(1179668016241243425)
XLA Ops:
  0.6 69.5 %shard_map.152 = (bf16[128,512]{1,0:T(8,128)(2,1)}, bf16[128,512]{1,0:T(8,128)(2,1)}, bf16[128,512]{1,0:T(8,128)(2,1)}, f32[128,128]{1,0:T(8,128)}, f32[128,128]...) custom-call(bf16[128,512]{1,0:T(8,128)(2,1)} %v_in.1, bf16[128,512]{1,0:T(8,128)(2,1)} %g_in.1, ...), custom_call_target="tpu_custom_call" | custom-call | tf_op jit(solution)/shard_map/pallas_call | solution.py:845
  70.1 1.9 %shard_map.153 = (bf16[128,512]{1,0:T(8,128)(2,1)}, bf16[128,512]{1,0:T(8,128)(2,1)}, bf16[128,512]{1,0:T(8,128)(2,1)}, f32[128,128]{1,0:T(8,128)}, f32[128,128]...) custom-call(bf16[128,512]{1,0:T(8,128)(2,1)} %get-tuple-element.16.refs_0_, ...), custom_call_target="tpu_custom_call" | custom-call | tf_op jit(solution)/shard_map/pallas_call | solution.py:857
